TPU v7x, 32 devices: a whole 2x2x4 slice. The times are simulated.
32 devices in a mesh: grp: 2 (over x), wide: 16 (over z, y, core).
Axes of the slice: x: 2, y: 2, z: 4, core: 2. Of those that a mesh axis runs over, the one named last changes fastest.
Arguments:
- voltages: bfloat16 [2048, 2, 8240], P(('grp', 'wide')), parts along dimension 0, may hold values from -6 to 6
- taps: float32 [4, 16], replicated, may hold values from -3 to 3
- flags: int32 [2048], P(('grp', 'wide')), parts along dimension 0, may hold values 0 or 1
- positions: float32 [2, 1024], replicated, may hold values from -20 to 20
- beam_index: int32 [512], P('grp'), parts along dimension 0, may hold values from 0 to 1023
Outputs:
- power: float32 [512, 16, 128], P(('grp', 'wide')), parts along dimension 0
There are 2 independent parts, one for each index of `grp`. A program takes and returns all parts, laid end to end along the dimension named above; an argument that names none is the same for every part. Nothing has to cross between parts.
Inputs may be any that keep to these rules, and one draw needn't show every extreme that they name: 1 keeps an antenna, 0 flags it.
All inputs are finite; a program needn't handle non-finite values. No bound on the sum of `flags` on one device may be relied on, other than what follows from the above.
Results may differ from a plain program's by a relative error of at most 0.0075.
Values may be sent and summed in bfloat16 or wider, within the bound.
A program may use at most 128 MiB of HBM per device.

v0:
```python
import functools
import math

import jax
import jax.numpy as jnp
import numpy as np
from jax import lax
from jax.experimental import pallas as pl
from jax.experimental.pallas import tpu as pltpu
from jax.sharding import PartitionSpec as P

ITERS = 2


damping = 0.5
grid_side = 32


def channelize(voltages, taps, flags):
    count = voltages.shape[0]
    chans = taps.shape[1]
    ntaps = taps.shape[0]
    total = voltages.shape[2] // chans - ntaps + 1
    samples = voltages.astype(jnp.float32).reshape(count, 2, total + ntaps - 1, chans)
    filtered = taps[0][None, None, None, :] * samples[:, :, 0:total, :]
    for tap in range(1, ntaps):
        filtered = filtered + taps[tap][None, None, None, :] * samples[:, :, tap : tap + total, :]
    branch = jnp.arange(chans, dtype=jnp.int32)
    angle = 2.0 * math.pi / chans * (branch[:, None] * branch[None, :] % chans).astype(jnp.float32)
    cosine = jnp.cos(angle)
    sine = jnp.sin(angle)
    high = lax.Precision.HIGHEST
    real_in = filtered[:, 0]
    imag_in = filtered[:, 1]
    real_out = jnp.einsum("asp,pc->acs", real_in, cosine, precision=high) + jnp.einsum(
        "asp,pc->acs", imag_in, sine, precision=high
    )
    imag_out = jnp.einsum("asp,pc->acs", imag_in, cosine, precision=high) - jnp.einsum(
        "asp,pc->acs", real_in, sine, precision=high
    )
    keep = flags.astype(jnp.float32)[:, None, None] / math.sqrt(chans)
    return jnp.stack([real_out * keep, imag_out * keep]).astype(jnp.bfloat16)


def steering(channel, positions, beam_index, chans):
    column = (beam_index % grid_side).astype(jnp.float32)
    row_cell = (beam_index // grid_side).astype(jnp.float32)
    east = (column + 0.5) / grid_side - 0.5
    north = (row_cell + 0.5) / grid_side - 0.5
    ratio = 1.0 + 0.5 * channel.astype(jnp.float32) / chans
    phase = (
        2.0
        * math.pi
        * ratio
        * (positions[0][:, None] * east[None, :] + positions[1][:, None] * north[None, :])
    )
    return (jnp.cos(phase), -jnp.sin(phase))


def form_beams(blocks, channel, positions, beam_index, total, chans):
    high = lax.Precision.HIGHEST
    cov_real = 0.0
    cov_imag = 0.0
    for block in blocks:
        left = jnp.concatenate([block[0], block[1]], axis=1)
        turned = jnp.concatenate([block[1], -block[0]], axis=1)
        cov_real = cov_real + jnp.dot(left, left.T, preferred_element_type=jnp.float32)
        cov_imag = cov_imag + jnp.dot(turned, left.T, preferred_element_type=jnp.float32)
    cov_real = cov_real / total
    cov_imag = cov_imag / total
    count = cov_real.shape[0]
    diagonal = jnp.diagonal(cov_real)
    loading = jnp.mean(diagonal) + 1e-05
    scaling = (damping / (diagonal + loading))[:, None]
    steer_real, steer_imag = steering(channel, positions, beam_index, chans)
    weight_real = scaling * steer_real
    weight_imag = scaling * steer_imag
    for sweep in range(ITERS):
        image_real = (
            jnp.dot(cov_real, weight_real, precision=high)
            - jnp.dot(cov_imag, weight_imag, precision=high)
            + loading * weight_real
        )
        image_imag = (
            jnp.dot(cov_real, weight_imag, precision=high)
            + jnp.dot(cov_imag, weight_real, precision=high)
            + loading * weight_imag
        )
        weight_real = weight_real + scaling * (steer_real - image_real)
        weight_imag = weight_imag + scaling * (steer_imag - image_imag)
    low_real = weight_real.astype(jnp.bfloat16)
    low_imag = weight_imag.astype(jnp.bfloat16)
    plain = jnp.concatenate([low_real, low_imag], axis=0)
    mixed = jnp.concatenate([low_real, -low_imag], axis=0)
    contract = (((0,), (0,)), ((), ()))
    reals = []
    imags = []
    for block in blocks:
        reals.append(
            lax.dot_general(
                plain,
                jnp.concatenate([block[0], block[1]], axis=0),
                contract,
                preferred_element_type=jnp.float32,
            )
        )
        imags.append(
            lax.dot_general(
                mixed,
                jnp.concatenate([block[1], block[0]], axis=0),
                contract,
                preferred_element_type=jnp.float32,
            )
        )
    norm_factor = 1.0 / math.sqrt(count)
    beams = (
        jnp.stack([jnp.concatenate(reals, axis=-1), jnp.concatenate(imags, axis=-1)]) * norm_factor
    )
    return beams.astype(jnp.bfloat16)


def detect(beams):
    floats = beams.astype(jnp.float32)
    energy = floats[:, 0] * floats[:, 0] + floats[:, 1] * floats[:, 1]
    shape = energy.shape
    return energy.reshape(shape[0], shape[1], shape[2] // 4, 4).sum(axis=-1)


def plain(voltages, taps, flags, positions, beam_index):
    spectra = channelize(voltages, taps, flags)
    chans = taps.shape[1]
    per_dev = chans // lax.axis_size("wide")
    first = lax.axis_index("wide") * per_dev
    total = spectra.shape[3]
    pieces = [lax.all_to_all(spectra, "wide", split_axis=2, concat_axis=1, tiled=True)]
    stacked = [jnp.moveaxis(piece, 2, 0) for piece in pieces]

    def one_channel(operands):
        offset, blocks = operands
        return form_beams(blocks, first + offset, positions, beam_index, total, chans)

    beams = lax.map(one_channel, (jnp.arange(per_dev, dtype=jnp.int32), stacked))
    result = lax.all_to_all(
        detect(beams).astype(jnp.bfloat16), "wide", split_axis=1, concat_axis=0, tiled=True
    ).astype(jnp.float32)
    return jnp.transpose(result, (1, 0, 2))


MESH = pl.DeviceIdType.MESH
LANES = 128
ROWS = 16
NT = (((1,), (1,)), ((), ()))


def cosine_turns(turns):
    frac = jnp.abs(turns - jnp.floor(turns + 0.5))
    x = (0.25 - frac) * (2.0 * math.pi)
    sq = x * x
    poly = -1.0 / 39916800.0
    for term in (1.0 / 362880.0, -1.0 / 5040.0, 1.0 / 120.0, -1.0 / 6.0, 1.0):
        poly = poly * sq + term
    return x * poly


def swap_halves(block):
    return pltpu.roll(block, LANES // 2, 1)


def kernel(
    volt_ref, order_ref, bank_ref, place_ref, cell_ref, out_ref,
    mixed, sent, spec, steer, weight, low, image, give, got,
    send_sem, recv_sem, own_sem, give_sem, got_sem,
    *, wide, total, chans, window, parts,
):
    me = lax.axis_index("wide")
    peers = wide - 1
    step = total // parts
    beams = cell_ref.shape[0]
    width = wide * LANES

    barrier = pltpu.get_barrier_semaphore()

    def greet(off, carry):
        pl.semaphore_signal(
            barrier, inc=1, device_id={"wide": lax.rem(me + off, wide)}, device_id_type=MESH
        )
        return carry

    lax.fori_loop(1, wide, greet, 0)

    mixed[...] = jnp.dot(
        order_ref[...], volt_ref[...], preferred_element_type=jnp.float32
    ).astype(jnp.bfloat16)

    def spectra_copy(part, other):
        rows = pl.ds(pl.multiple_of(part * step, step), step)
        return pltpu.make_async_remote_copy(
            src_ref=sent.at[other, rows, :],
            dst_ref=spec.at[rows, pl.ds(pl.multiple_of(me * LANES, LANES), LANES)],
            send_sem=send_sem.at[part, other],
            recv_sem=recv_sem.at[part, me],
            device_id={"wide": other},
            device_id_type=MESH,
        )

    def arrival(part, other):
        rows = pl.ds(pl.multiple_of(part * step, step), step)
        return pltpu.make_async_remote_copy(
            src_ref=sent.at[other, rows, :],
            dst_ref=spec.at[rows, pl.ds(pl.multiple_of(other * LANES, LANES), LANES)],
            send_sem=send_sem.at[part, other],
            recv_sem=recv_sem.at[part, other],
            device_id={"wide": other},
            device_id_type=MESH,
        )

    def own_copy(part):
        rows = pl.ds(pl.multiple_of(part * step, step), step)
        return pltpu.make_async_copy(
            sent.at[me, rows, :],
            spec.at[rows, pl.ds(pl.multiple_of(me * LANES, LANES), LANES)],
            own_sem.at[part],
        )

    hop = ROWS * chans
    pairs = step // (2 * ROWS)

    def channelize_pair(pair, carry):
        start = pl.multiple_of(pair * (2 * hop), LANES)
        acc = jnp.zeros((hop, 2 * LANES), jnp.float32)
        for half in range(2):
            rows = slice(half * LANES, (half + 1) * LANES)
            both = jnp.concatenate(
                [
                    mixed[rows, pl.ds(start, window)],
                    mixed[rows, pl.ds(pl.multiple_of(start + hop, LANES), window)],
                ],
                axis=0,
            )
            for piece in range(2):
                acc = acc + lax.dot_general(
                    bank_ref[2 * half + piece], both, NT, preferred_element_type=jnp.float32
                )
        rounded = acc.astype(jnp.bfloat16)
        row = pl.multiple_of(pair * (2 * ROWS), ROWS)
        sent[:, pl.ds(row, ROWS), :] = rounded[:, :LANES].reshape(chans, ROWS, LANES)
        row = pl.multiple_of(row + ROWS, ROWS)
        sent[:, pl.ds(row, ROWS), :] = rounded[:, LANES:].reshape(chans, ROWS, LANES)
        return carry

    for part in range(parts):
        lax.fori_loop(part * pairs, (part + 1) * pairs, channelize_pair, 0)
        if part == 0:
            pl.semaphore_wait(barrier, peers)

        def ship(off, carry, part=part):
            spectra_copy(part, lax.rem(me + off, wide)).start()
            return carry

        lax.fori_loop(1, wide, ship, 0)
        own_copy(part).start()

    ratio = 1.0 + 0.5 * me.astype(jnp.float32) / chans
    east = cell_ref[:, 0:1] * ratio
    north = cell_ref[:, 1:2] * ratio

    def steer_block(block, carry):
        lanes = pl.ds(pl.multiple_of(block * LANES, LANES), LANES)
        turns = east * place_ref[0:1, lanes] + north * place_ref[1:2, lanes]
        steer[:, lanes] = cosine_turns(turns + place_ref[2:3, lanes])
        return carry

    lax.fori_loop(0, wide, steer_block, 0)

    power = jnp.zeros((8, width), jnp.float32)
    for part in range(parts):

        def take(off, carry, part=part):
            arrival(part, lax.rem(me + off, wide)).wait_recv()
            return carry

        lax.fori_loop(1, wide, take, 0)
        own_copy(part).wait()
        for row in range(part * step, (part + 1) * step, ROWS):
            block = spec[row : row + ROWS, :].astype(jnp.float32)
            block = block * block
            power = power + (block[:8] + block[8:])
    power = jnp.sum(power, axis=0, keepdims=True) * (1.0 / total)
    loading = jnp.sum(power) / (width // 2) + 1e-05
    lane = lax.broadcasted_iota(jnp.int32, (1, LANES), 1)
    sign = jnp.where(lane < LANES // 2, 1.0, -1.0)

    scales = []
    for block in range(wide):
        piece = power[:, block * LANES : (block + 1) * LANES]
        piece = piece + swap_halves(jnp.broadcast_to(piece, (8, LANES)))[0:1]
        scales.append(0.5 / (piece + loading))

    def keep_low(lanes, value):
        low[:beams, lanes] = value.astype(jnp.bfloat16)
        low[beams:, lanes] = (swap_halves(value) * sign).astype(jnp.bfloat16)

    for block in range(wide):
        lanes = slice(block * LANES, (block + 1) * LANES)
        value = scales[block] * steer[:, lanes]
        weight[:, lanes] = value
        keep_low(lanes, value)

    half_rows = total // 2

    def project(store):
        for cut in range(2):
            rows = slice(cut * half_rows, (cut + 1) * half_rows)
            store(
                rows,
                lax.dot_general(
                    low[...], spec[rows, :], NT, preferred_element_type=jnp.float32
                ),
            )

    def keep_image(rows, value):
        image[:, rows] = value.astype(jnp.bfloat16)

    for sweep in range(ITERS):
        project(keep_image)
        for duo in range(wide // 2):
            span = slice(2 * duo * LANES, (2 * duo + 2) * LANES)
            back = jnp.dot(image[...], spec[:, span], preferred_element_type=jnp.float32)
            for side in range(2):
                block = 2 * duo + side
                lanes = slice(block * LANES, (block + 1) * LANES)
                cols = slice(side * LANES, (side + 1) * LANES)
                applied = back[:beams, cols] - sign * swap_halves(back[beams:, cols])
                value = weight[:, lanes]
                value = value + scales[block] * (
                    steer[:, lanes] - (applied * (1.0 / total) + loading * value)
                )
                if sweep < ITERS - 1:
                    weight[:, lanes] = value
                keep_low(lanes, value)

    group = total // 4
    share = give.shape[1]
    sums = jnp.zeros((beams, group), jnp.float32)
    for cut in range(2):
        rows = slice(cut * half_rows, (cut + 1) * half_rows)
        value = lax.dot_general(low[...], spec[rows, :], NT, preferred_element_type=jnp.float32)
        energy = value[:beams] * value[:beams] + value[beams:] * value[beams:]
        energy = energy * (2.0 / width)
        top = energy.astype(jnp.bfloat16)
        rest = (energy - top.astype(jnp.float32)).astype(jnp.bfloat16)
        source = lax.broadcasted_iota(jnp.int32, (half_rows, group), 0) + cut * half_rows
        target = lax.broadcasted_iota(jnp.int32, (half_rows, group), 1) * 4
        pick = jnp.where((source >= target) & (source < target + 4), 1.0, 0.0)
        pick = pick.astype(jnp.bfloat16)
        sums = sums + jnp.dot(top, pick, preferred_element_type=jnp.float32)
        sums = sums + jnp.dot(rest, pick, preferred_element_type=jnp.float32)
    give[...] = sums.astype(jnp.bfloat16).reshape(wide, share, group)

    def power_copy(other, slot):
        return pltpu.make_async_remote_copy(
            src_ref=give.at[other],
            dst_ref=got.at[slot],
            send_sem=give_sem.at[other],
            recv_sem=got_sem.at[slot],
            device_id={"wide": other},
            device_id_type=MESH,
        )

    def hand(off, carry):
        power_copy(lax.rem(me + off, wide), me).start()
        return carry

    lax.fori_loop(1, wide, hand, 0)
    mine = pltpu.make_async_copy(give.at[me], got.at[me], own_sem.at[parts])
    mine.start()

    for part in range(parts):

        def settle(off, carry, part=part):
            spectra_copy(part, lax.rem(me + off, wide)).wait_send()
            return carry

        lax.fori_loop(1, wide, settle, 0)

    def close(off, carry):
        other = lax.rem(me + off, wide)
        power_copy(other, other).wait_recv()
        return carry

    lax.fori_loop(1, wide, close, 0)
    mine.wait()
    for channel in range(chans):
        out_ref[:, channel, :] = got[channel].astype(jnp.float32)

    def done(off, carry):
        power_copy(lax.rem(me + off, wide), me).wait_send()
        return carry

    lax.fori_loop(1, wide, done, 0)


def fused(voltages, taps, flags, positions, beam_index):
    wide = lax.axis_size("wide")
    count, _, length = voltages.shape
    ntaps, chans = taps.shape
    total = length // chans - ntaps + 1
    beams = beam_index.shape[0]
    hop = ROWS * chans
    window = -(-(ROWS + ntaps - 1) * chans // LANES) * LANES
    padded = (total // ROWS - 1) * hop + window
    parts = 4
    step = total // parts

    volt = jnp.pad(voltages.reshape(2 * count, length), ((0, 0), (0, padded - length)))

    antenna = np.arange(count)
    base = np.zeros((4 * count, 2 * count), np.float32)
    base[antenna, 2 * antenna] = 1.0
    base[count + antenna, 2 * antenna + 1] = 1.0
    base[2 * count + antenna, 2 * antenna + 1] = 1.0
    base[3 * count + antenna, 2 * antenna] = -1.0
    keep = jnp.repeat(flags.astype(jnp.float32), 2)
    order = (jnp.asarray(base) * keep[None, :]).astype(jnp.bfloat16)

    branch = np.arange(chans)
    angle = 2.0 * math.pi / chans * (branch[:, None] * branch[None, :] % chans)
    waves = (np.stack([np.cos(angle), np.sin(angle)]) / math.sqrt(chans)).astype(np.float32)
    slots = window // chans
    delay = np.arange(slots)[None, :] - np.arange(ROWS)[:, None]
    filt = 0.0
    for tap in range(ntaps):
        here = jnp.asarray((delay == tap).astype(np.float32))
        filt = filt + here[:, :, None] * taps[tap][None, None, :]
    bank = jnp.asarray(waves)[:, :, None, None, :] * filt[None, None]
    bank = bank.reshape(2, hop, window)
    top = bank.astype(jnp.bfloat16)
    rest = (bank - top.astype(jnp.float32)).astype(jnp.bfloat16)
    bank = jnp.stack([top, rest], axis=1).reshape(4, hop, window)

    spread = jnp.broadcast_to(positions.reshape(2, wide, 1, count), (2, wide, 2, count))
    quarter = np.zeros((1, wide, 2, count), np.float32)
    quarter[:, :, 1] = 0.25
    place = jnp.concatenate([spread, jnp.asarray(quarter)]).reshape(3, wide * 2 * count)
    column = (beam_index % grid_side).astype(jnp.float32)
    row_cell = (beam_index // grid_side).astype(jnp.float32)
    cell = jnp.stack(
        [(column + 0.5) / grid_side - 0.5, (row_cell + 0.5) / grid_side - 0.5], axis=1
    )

    share = beams // wide
    width = wide * LANES
    vmem = pl.BlockSpec(memory_space=pltpu.VMEM)
    return pl.pallas_call(
        functools.partial(
            kernel, wide=wide, total=total, chans=chans, window=window, parts=parts
        ),
        out_shape=jax.ShapeDtypeStruct((share, chans, total // 4), jnp.float32),
        in_specs=[vmem] * 5,
        out_specs=vmem,
        scratch_shapes=[
            pltpu.VMEM((2 * LANES, padded), jnp.bfloat16),
            pltpu.VMEM((chans, total, LANES), jnp.bfloat16),
            pltpu.VMEM((total, width), jnp.bfloat16),
            pltpu.VMEM((beams, width), jnp.float32),
            pltpu.VMEM((beams, width), jnp.float32),
            pltpu.VMEM((2 * beams, width), jnp.bfloat16),
            pltpu.VMEM((2 * beams, total), jnp.bfloat16),
            pltpu.VMEM((wide, share, total // 4), jnp.bfloat16),
            pltpu.VMEM((chans, share, total // 4), jnp.bfloat16),
            pltpu.SemaphoreType.DMA((parts, wide)),
            pltpu.SemaphoreType.DMA((parts, wide)),
            pltpu.SemaphoreType.DMA((parts + 1,)),
            pltpu.SemaphoreType.DMA((wide,)),
            pltpu.SemaphoreType.DMA((wide,)),
        ],
        compiler_params=pltpu.CompilerParams(
            collective_id=0, has_side_effects=True, vmem_limit_bytes=48 * 2**20
        ),
    )(volt, order, bank, place, cell)


def fits(voltages, taps, beam_index, wide):
    count, _, length = voltages.shape
    ntaps, chans = taps.shape
    total = length // chans - ntaps + 1
    return (
        2 * count == LANES
        and chans == wide
        and (ROWS * chans) % LANES == 0
        and wide % 2 == 0
        and total % 256 == 0
        and beam_index.shape[0] % (ROWS * wide) == 0
        and (total // 4) % LANES == 0
    )


def local(voltages, taps, flags, positions, beam_index):
    if fits(voltages, taps, beam_index, lax.axis_size("wide")):
        return fused(voltages, taps, flags, positions, beam_index)
    return plain(voltages, taps, flags, positions, beam_index)


def solution(mesh):
    in_specs = (P(("grp", "wide"), None, None), P(), P(("grp", "wide")), P(), P("grp"))
    out_specs = P(("grp", "wide"), None, None)
    return jax.shard_map(local, mesh=mesh, in_specs=in_specs, out_specs=out_specs, check_vma=False)
```

profile of v0, /device:TPU:0, one launch (start us, length us, event | category | flops | bytes accessed | tf_op | source)
XLA Modules:
  0.0 88.2 jit_solution(7841148332317264747)
XLA Ops:
  0.0 0.8 slice_bitcast_fusion.3
  0.8 1.0 %multiply_add_fusion = f32[16,24,16]{2,1,0:T(8,128)S(1)} fusion(f32[16]{0:T(128)S(1)} %get-tuple-element.9, f32[16,24]{1,0:T(8,128)} %constant.58.clone, f32[16]{0:T(128)S(1)} %get-tuple-element.10, f32[16,24]{1,0:T(8,128)} %constant.57.clone, f32[16]{0:T(128)S(1)} %get-tuple-element.8, f32[16,24]{1,0:T(8,128)} %constant.56.clone, ...), kind=kLoop, calls=%fused_computation.3 | loop fusion | flops 43008 | bytes 30976 | tf_op jit(solution)/shard_map/add | solution.py:434
  1.9 1.9 %mul.138 = f32[16,16,24,16]{3,2,1,0:T(8,128)} broadcast(f32[16,24,16]{2,1,0:T(8,128)S(1)} %multiply_add_fusion), dimensions={1,2,3} | broadcast | bytes 417792 | tf_op jit(solution)/shard_map/mul | solution.py:435
  3.8 2.5 %mul.139 = f32[256,384]{1,0:T(8,128)S(1)} reshape(f32[16,16,24,16]{3,2,1,0:T(8,128)} %mul.138) | data formatting | bytes 786432 | tf_op jit(solution)/shard_map/mul | solution.py:435
  6.3 0.0 copy-done.2
  6.3 3.1 %mul.120 = f32[2,16,16,24,16]{4,3,2,1,0:T(8,128)} broadcast(f32[2,16,16]{2,1,0:T(8,128)S(1)} %copy-done.2), dimensions={0,1,4} | broadcast | bytes 788480 | tf_op jit(solution)/shard_map/mul | solution.py:435
  9.4 4.4 %mul.121 = f32[2,1,256,384]{3,2,0,1:T(8,128)S(1)} reshape(f32[2,16,16,24,16]{4,3,2,1,0:T(8,128)} %mul.120) | data formatting | bytes 1572864 | tf_op jit(solution)/shard_map/mul | solution.py:435
  13.8 0.0 copy-start.5
  13.8 0.1 multiply_convert_fusion
  13.9 0.0 copy-start
  13.9 0.1 pad_maximum_fusion
  14.0 0.1 copy.16
  14.1 0.3 copy-done.5
  14.5 0.1 copy.17.cell_ref
  14.6 0.9 %copy-done = bf16[64,2,8240]{2,1,0:T(2,128)(2,1)S(1)} copy-done((bf16[64,2,8240]{2,1,0:T(2,128)(2,1)S(1)}, bf16[64,2,8240]{2,1,0:T(2,128)(2,1)}, u32[]{:S(2)}) %copy-start) | copy-done | bytes 2109464
  15.5 2.8 %reshape.57 = bf16[128,8240]{1,0:T(8,128)(2,1)} reshape(bf16[64,2,8240]{2,1,0:T(2,128)(2,1)S(1)} %copy-done) | data formatting | bytes 4218880 | tf_op jit(solution)/shard_map/reshape | solution.py:415
  18.3 1.8 %pad.4.volt_ref = bf16[128,8320]{1,0:T(8,128)(2,1)S(1)} pad(bf16[128,8240]{1,0:T(8,128)(2,1)} %reshape.57, bf16[]{:T(256)} %constant.44.clone.1), padding=0_0x0_80 | pad | bytes 4239362 | tf_op jit(solution)/shard_map/jit(_pad)/pad | solution.py:415
  20.1 0.0 copy-done.4
  20.1 0.1 broadcast_in_dim.7
  20.3 0.1 reshape.59.place_ref
  20.4 0.1 broadcast_in_dim.6
  20.5 0.1 mul.117
  20.7 66.9 %shard_map.118 = f32[16,16,128]{2,1,0:T(8,128)S(1)} custom-call(bf16[128,8320]{1,0:T(8,128)(2,1)S(1)} %pad.4.volt_ref, bf16[256,128]{1,0:T(8,128)(2,1)S(1)} %multiply_convert_fusion.1.order_ref, bf16[4,256,384]{2,1,0:T(8,128)(2,1)S(1)} %bitcast.15, f32[3,2048]{1,0:T(4,128)S(1)} %reshape.59.place_ref, f32[256,2]{1,0:T(8,128)S(1)} %copy.17.cell_ref), custom_call_target="tpu_custom_call" | custom-call | tf_op jit(solution)/shard_map/pallas_call | solution.py:454
  87.6 0.7 copy.19
  (14 shorter events, 0.1 us)
Async XLA Ops:
  3.8 2.5 %copy-start.2 = (f32[2,16,16]{2,1,0:T(8,128)S(1)}, f32[2,16,16]{2,1,0:T(8,128)}, u32[]{:S(2)}) copy-start(f32[2,16,16]{2,1,0:T(8,128)} %constant.59.clone) | copy-start | bytes 6148
  13.8 0.7 copy-start.5
  13.9 1.6 %copy-start = (bf16[64,2,8240]{2,1,0:T(2,128)(2,1)S(1)}, bf16[64,2,8240]{2,1,0:T(2,128)(2,1)}, u32[]{:S(2)}) copy-start(bf16[64,2,8240]{2,1,0:T(2,128)(2,1)} %param.12) | copy-start | bytes 6328324
  18.3 1.8 %copy-start.4 = (f32[2,1024]{1,0:T(2,128)S(1)}, f32[2,1024]{1,0:T(2,128)}, u32[]{:S(2)}) copy-start(f32[2,1024]{1,0:T(2,128)} %param.15) | copy-start | bytes 24580
  18.3 1.9 %copy-start.3 = (f32[1,16,2,64]{3,2,1,0:T(2,128)S(1)}, f32[1,16,2,64]{3,2,1,0:T(2,128)}, u32[]{:S(2)}) copy-start(f32[1,16,2,64]{3,2,1,0:T(2,128)} %constant.60.clone) | copy-start | bytes 24580
  18.3 2.1 %copy-start.6 = (s32[64]{0:T(128)S(1)}, s32[64]{0:T(128)}, u32[]{:S(2)}) copy-start(s32[64]{0:T(128)} %param.14) | copy-start | bytes 772
  18.3 2.3 %copy-start.1 = (f32[256,128]{1,0:T(8,128)S(1)}, f32[256,128]{1,0:T(8,128)}, u32[]{:S(2)}) copy-start(f32[256,128]{1,0:T(8,128)} %constant.54.clone) | copy-start | bytes 393220
where the time goes:
time: 88.5 us; the launch traced here: 88.2 us
  Pallas kernels  66.9 us (76%)
  local copies, waits for them, and re-layouts  19.9 us (22%)
  other arithmetic  1.29 us (1%)
    pallas_call x1, Pallas kernels, fused(): pl.pallas_call(functools.partial(kernel, wide=wide, total=total, chans=ch...  66.9 us
    mul x4, local copies, waits for them, and re-layouts, fused(): bank = jnp.asarray(waves)[:, :, None, None, :] * filt[None, None]  11.9 us
    reshape x1, local copies, waits for them, and re-layouts, fused(): voltages.reshape(2 * count, length)  2.81 us
    unnamed x15, local copies, waits for them, and re-layouts  1.92 us
    pad x1, local copies, waits for them, and re-layouts, fused(): jnp.pad(voltages.reshape(2 * count, length), ((0, 0), (0, padded - length)))  1.8 us

commit v1 on v0

--- a/solution.py
+++ b/solution.py
@@ -167,9 +167,10 @@
 
 
 def kernel(
-    volt_ref, order_ref, bank_ref, place_ref, cell_ref, out_ref,
-    mixed, sent, spec, steer, weight, low, image, give, got,
-    send_sem, recv_sem, own_sem, give_sem, got_sem,
+    volt_ref, order_ref, wave_ref, taps_ref, place_ref, cell_ref, out_ref,
+    bank, mixed, sent, spec, steer, weight, low, image, applied, scale,
+    tell, told, give, got,
+    send_sem, recv_sem, own_sem, tell_sem, told_sem, give_sem, got_sem,
     *, wide, total, chans, window, parts,
 ):
     me = lax.axis_index("wide")
@@ -177,53 +178,79 @@
     step = total // parts
     beams = cell_ref.shape[0]
     width = wide * LANES
+    hop = ROWS * chans
+    length = volt_ref.shape[2]
+    ntaps = taps_ref.shape[0]
 
     barrier = pltpu.get_barrier_semaphore()
 
-    def greet(off, carry):
-        pl.semaphore_signal(
-            barrier, inc=1, device_id={"wide": lax.rem(me + off, wide)}, device_id_type=MESH
-        )
-        return carry
-
-    lax.fori_loop(1, wide, greet, 0)
-
-    mixed[...] = jnp.dot(
-        order_ref[...], volt_ref[...], preferred_element_type=jnp.float32
-    ).astype(jnp.bfloat16)
-
-    def spectra_copy(part, other):
-        rows = pl.ds(pl.multiple_of(part * step, step), step)
+    def everyone(act):
+        def body(off, carry):
+            act(lax.rem(me + off, wide))
+            return carry
+
+        lax.fori_loop(1, wide, body, 0)
+
+    everyone(
+        lambda other: pl.semaphore_signal(
+            barrier, inc=1, device_id={"wide": other}, device_id_type=MESH
+        )
+    )
+
+    slot = lax.broadcasted_iota(jnp.int32, (ROWS, window), 1) // chans
+    delay = slot - lax.broadcasted_iota(jnp.int32, (ROWS, window), 0)
+    filt = jnp.zeros((ROWS, window), jnp.float32)
+    for tap in range(ntaps):
+        filt = filt + jnp.where(delay == tap, taps_ref[tap : tap + 1, :], 0.0)
+    for half in range(2):
+        for channel in range(chans):
+            rows = slice(channel * ROWS, (channel + 1) * ROWS)
+            entry = wave_ref[half, channel : channel + 1, :] * filt
+            top = entry.astype(jnp.bfloat16)
+            bank[2 * half, rows, :] = top
+            bank[2 * half + 1, rows, :] = (entry - top.astype(jnp.float32)).astype(jnp.bfloat16)
+
+    def mix(start, size):
+        volt = volt_ref[:, :, start : start + size].reshape(LANES, size)
+        mixed[:, start : start + size] = jnp.dot(
+            order_ref[...], volt, preferred_element_type=jnp.float32
+        ).astype(jnp.bfloat16)
+
+    def rows_of(part):
+        return pl.ds(pl.multiple_of(part * step, step), step)
+
+    def lanes_of(block):
+        return pl.ds(pl.multiple_of(block * LANES, LANES), LANES)
+
+    def spectra_copy(part, other, owner):
         return pltpu.make_async_remote_copy(
-            src_ref=sent.at[other, rows, :],
-            dst_ref=spec.at[rows, pl.ds(pl.multiple_of(me * LANES, LANES), LANES)],
+            src_ref=sent.at[other, rows_of(part), :],
+            dst_ref=spec.at[rows_of(part), lanes_of(owner)],
             send_sem=send_sem.at[part, other],
-            recv_sem=recv_sem.at[part, me],
+            recv_sem=recv_sem.at[part, owner],
             device_id={"wide": other},
             device_id_type=MESH,
         )
 
-    def arrival(part, other):
-        rows = pl.ds(pl.multiple_of(part * step, step), step)
+    def own_copy(part):
+        return pltpu.make_async_copy(
+            sent.at[me, rows_of(part), :],
+            spec.at[rows_of(part), lanes_of(me)],
+            own_sem.at[part],
+        )
+
+    def tell_copy(other, owner):
         return pltpu.make_async_remote_copy(
-            src_ref=sent.at[other, rows, :],
-            dst_ref=spec.at[rows, pl.ds(pl.multiple_of(other * LANES, LANES), LANES)],
-            send_sem=send_sem.at[part, other],
-            recv_sem=recv_sem.at[part, other],
+            src_ref=tell.at[other],
+            dst_ref=told.at[owner],
+            send_sem=tell_sem.at[other],
+            recv_sem=told_sem.at[owner],
             device_id={"wide": other},
             device_id_type=MESH,
         )
 
-    def own_copy(part):
-        rows = pl.ds(pl.multiple_of(part * step, step), step)
-        return pltpu.make_async_copy(
-            sent.at[me, rows, :],
-            spec.at[rows, pl.ds(pl.multiple_of(me * LANES, LANES), LANES)],
-            own_sem.at[part],
-        )
-
-    hop = ROWS * chans
     pairs = step // (2 * ROWS)
+    tell[...] = jnp.zeros_like(tell)
 
     def channelize_pair(pair, carry):
         start = pl.multiple_of(pair * (2 * hop), LANES)
@@ -239,25 +266,36 @@
             )
             for piece in range(2):
                 acc = acc + lax.dot_general(
-                    bank_ref[2 * half + piece], both, NT, preferred_element_type=jnp.float32
+                    bank[2 * half + piece], both, NT, preferred_element_type=jnp.float32
                 )
         rounded = acc.astype(jnp.bfloat16)
-        row = pl.multiple_of(pair * (2 * ROWS), ROWS)
-        sent[:, pl.ds(row, ROWS), :] = rounded[:, :LANES].reshape(chans, ROWS, LANES)
-        row = pl.multiple_of(row + ROWS, ROWS)
-        sent[:, pl.ds(row, ROWS), :] = rounded[:, LANES:].reshape(chans, ROWS, LANES)
+        for side in range(2):
+            row = pl.multiple_of(pair * (2 * ROWS) + side * ROWS, ROWS)
+            block = rounded[:, side * LANES : (side + 1) * LANES].reshape(chans, ROWS, LANES)
+            sent[:, pl.ds(row, ROWS), :] = block
+            block = block.astype(jnp.float32)
+            block = block * block
+            tell[...] += block[:, :8] + block[:, 8:]
         return carry
 
+    tail = length // LANES * LANES
+    mixed[:, tail:] = jnp.zeros((2 * LANES, mixed.shape[1] - tail), jnp.bfloat16)
+    over = window - hop
+    reach = 0
     for part in range(parts):
+        upto = min((part + 1) * step * chans + over, length)
+        mix(reach, upto - reach)
+        reach = upto
         lax.fori_loop(part * pairs, (part + 1) * pairs, channelize_pair, 0)
         if part == 0:
             pl.semaphore_wait(barrier, peers)
-
-        def ship(off, carry, part=part):
-            spectra_copy(part, lax.rem(me + off, wide)).start()
-            return carry
-
-        lax.fori_loop(1, wide, ship, 0)
+            everyone(lambda other: spectra_copy(0, other, me).start())
+            own_copy(0).start()
+    everyone(lambda other: tell_copy(other, me).start())
+    own_tell = pltpu.make_async_copy(tell.at[me], told.at[me], own_sem.at[parts])
+    own_tell.start()
+    for part in range(1, parts):
+        everyone(lambda other, part=part: spectra_copy(part, other, me).start())
         own_copy(part).start()
 
     ratio = 1.0 + 0.5 * me.astype(jnp.float32) / chans
@@ -265,86 +303,85 @@
     north = cell_ref[:, 1:2] * ratio
 
     def steer_block(block, carry):
-        lanes = pl.ds(pl.multiple_of(block * LANES, LANES), LANES)
+        lanes = lanes_of(block)
         turns = east * place_ref[0:1, lanes] + north * place_ref[1:2, lanes]
         steer[:, lanes] = cosine_turns(turns + place_ref[2:3, lanes])
         return carry
 
     lax.fori_loop(0, wide, steer_block, 0)
 
-    power = jnp.zeros((8, width), jnp.float32)
-    for part in range(parts):
-
-        def take(off, carry, part=part):
-            arrival(part, lax.rem(me + off, wide)).wait_recv()
-            return carry
-
-        lax.fori_loop(1, wide, take, 0)
-        own_copy(part).wait()
-        for row in range(part * step, (part + 1) * step, ROWS):
-            block = spec[row : row + ROWS, :].astype(jnp.float32)
-            block = block * block
-            power = power + (block[:8] + block[8:])
-    power = jnp.sum(power, axis=0, keepdims=True) * (1.0 / total)
-    loading = jnp.sum(power) / (width // 2) + 1e-05
+    everyone(lambda other: tell_copy(other, other).wait_recv())
+    own_tell.wait()
     lane = lax.broadcasted_iota(jnp.int32, (1, LANES), 1)
     sign = jnp.where(lane < LANES // 2, 1.0, -1.0)
-
-    scales = []
+    power = jnp.sum(told[...], axis=1, keepdims=True) * (1.0 / total)
+    loading = jnp.sum(power) / (width // 2) + 1e-05
     for block in range(wide):
-        piece = power[:, block * LANES : (block + 1) * LANES]
-        piece = piece + swap_halves(jnp.broadcast_to(piece, (8, LANES)))[0:1]
-        scales.append(0.5 / (piece + loading))
+        piece = jnp.broadcast_to(power[block], (8, LANES))
+        piece = piece + swap_halves(piece)
+        scale[:, block * LANES : (block + 1) * LANES] = 0.5 / (piece + loading)
 
     def keep_low(lanes, value):
         low[:beams, lanes] = value.astype(jnp.bfloat16)
         low[beams:, lanes] = (swap_halves(value) * sign).astype(jnp.bfloat16)
 
-    for block in range(wide):
-        lanes = slice(block * LANES, (block + 1) * LANES)
-        value = scales[block] * steer[:, lanes]
+    def first_block(block, carry):
+        lanes = lanes_of(block)
+        value = scale[0:1, lanes] * steer[:, lanes]
         weight[:, lanes] = value
         keep_low(lanes, value)
-
-    half_rows = total // 2
-
-    def project(store):
-        for cut in range(2):
-            rows = slice(cut * half_rows, (cut + 1) * half_rows)
-            store(
-                rows,
-                lax.dot_general(
-                    low[...], spec[rows, :], NT, preferred_element_type=jnp.float32
-                ),
-            )
-
-    def keep_image(rows, value):
-        image[:, rows] = value.astype(jnp.bfloat16)
-
-    for sweep in range(ITERS):
-        project(keep_image)
-        for duo in range(wide // 2):
-            span = slice(2 * duo * LANES, (2 * duo + 2) * LANES)
-            back = jnp.dot(image[...], spec[:, span], preferred_element_type=jnp.float32)
+        return carry
+
+    lax.fori_loop(0, wide, first_block, 0)
+
+    def project(rows):
+        return lax.dot_general(low[...], spec[rows, :], NT, preferred_element_type=jnp.float32)
+
+    def back_project(rows, last, sweep, first):
+        def duo_block(duo, carry):
+            span = pl.ds(pl.multiple_of(duo * (2 * LANES), 2 * LANES), 2 * LANES)
+            back = jnp.dot(image[:, rows], spec[rows, span], preferred_element_type=jnp.float32)
             for side in range(2):
-                block = 2 * duo + side
-                lanes = slice(block * LANES, (block + 1) * LANES)
+                lanes = lanes_of(2 * duo + side)
                 cols = slice(side * LANES, (side + 1) * LANES)
-                applied = back[:beams, cols] - sign * swap_halves(back[beams:, cols])
+                fresh = back[:beams, cols] - sign * swap_halves(back[beams:, cols])
+                if not first:
+                    fresh = applied[:, lanes] + fresh
+                if not last:
+                    applied[:, lanes] = fresh
+                    continue
                 value = weight[:, lanes]
-                value = value + scales[block] * (
-                    steer[:, lanes] - (applied * (1.0 / total) + loading * value)
+                value = value + scale[0:1, lanes] * (
+                    steer[:, lanes] - (fresh * (1.0 / total) + loading * value)
                 )
                 if sweep < ITERS - 1:
                     weight[:, lanes] = value
                 keep_low(lanes, value)
+            return carry
+
+        lax.fori_loop(0, wide // 2, duo_block, 0)
+
+    groups = [(0, 2), (2, 3), (3, 4)]
+    for begin, end in groups:
+        for part in range(begin, end):
+            everyone(lambda other, part=part: spectra_copy(part, other, other).wait_recv())
+            own_copy(part).wait()
+        rows = slice(begin * step, end * step)
+        image[:, rows] = project(rows).astype(jnp.bfloat16)
+        back_project(rows, end == parts, 0, begin == 0)
+
+    half_rows = total // 2
+    halves = [slice(cut * half_rows, (cut + 1) * half_rows) for cut in range(2)]
+    for sweep in range(1, ITERS):
+        for rows in halves:
+            image[:, rows] = project(rows).astype(jnp.bfloat16)
+        back_project(slice(0, total), True, sweep, True)
 
     group = total // 4
     share = give.shape[1]
     sums = jnp.zeros((beams, group), jnp.float32)
-    for cut in range(2):
-        rows = slice(cut * half_rows, (cut + 1) * half_rows)
-        value = lax.dot_general(low[...], spec[rows, :], NT, preferred_element_type=jnp.float32)
+    for cut, rows in enumerate(halves):
+        value = project(rows)
         energy = value[:beams] * value[:beams] + value[beams:] * value[beams:]
         energy = energy * (2.0 / width)
         top = energy.astype(jnp.bfloat16)
@@ -357,47 +394,27 @@
         sums = sums + jnp.dot(rest, pick, preferred_element_type=jnp.float32)
     give[...] = sums.astype(jnp.bfloat16).reshape(wide, share, group)
 
-    def power_copy(other, slot):
+    def power_copy(other, owner):
         return pltpu.make_async_remote_copy(
             src_ref=give.at[other],
-            dst_ref=got.at[slot],
+            dst_ref=got.at[owner],
             send_sem=give_sem.at[other],
-            recv_sem=got_sem.at[slot],
+            recv_sem=got_sem.at[owner],
             device_id={"wide": other},
             device_id_type=MESH,
         )
 
-    def hand(off, carry):
-        power_copy(lax.rem(me + off, wide), me).start()
-        return carry
-
-    lax.fori_loop(1, wide, hand, 0)
-    mine = pltpu.make_async_copy(give.at[me], got.at[me], own_sem.at[parts])
+    everyone(lambda other: power_copy(other, me).start())
+    mine = pltpu.make_async_copy(give.at[me], got.at[me], own_sem.at[parts + 1])
     mine.start()
-
     for part in range(parts):
-
-        def settle(off, carry, part=part):
-            spectra_copy(part, lax.rem(me + off, wide)).wait_send()
-            return carry
-
-        lax.fori_loop(1, wide, settle, 0)
-
-    def close(off, carry):
-        other = lax.rem(me + off, wide)
-        power_copy(other, other).wait_recv()
-        return carry
-
-    lax.fori_loop(1, wide, close, 0)
+        everyone(lambda other, part=part: spectra_copy(part, other, me).wait_send())
+    everyone(lambda other: tell_copy(other, me).wait_send())
+    everyone(lambda other: power_copy(other, other).wait_recv())
     mine.wait()
     for channel in range(chans):
         out_ref[:, channel, :] = got[channel].astype(jnp.float32)
-
-    def done(off, carry):
-        power_copy(lax.rem(me + off, wide), me).wait_send()
-        return carry
-
-    lax.fori_loop(1, wide, done, 0)
+    everyone(lambda other: power_copy(other, me).wait_send())
 
 
 def fused(voltages, taps, flags, positions, beam_index):
@@ -410,9 +427,6 @@
     window = -(-(ROWS + ntaps - 1) * chans // LANES) * LANES
     padded = (total // ROWS - 1) * hop + window
     parts = 4
-    step = total // parts
-
-    volt = jnp.pad(voltages.reshape(2 * count, length), ((0, 0), (0, padded - length)))
 
     antenna = np.arange(count)
     base = np.zeros((4 * count, 2 * count), np.float32)
@@ -425,18 +439,9 @@
 
     branch = np.arange(chans)
     angle = 2.0 * math.pi / chans * (branch[:, None] * branch[None, :] % chans)
-    waves = (np.stack([np.cos(angle), np.sin(angle)]) / math.sqrt(chans)).astype(np.float32)
-    slots = window // chans
-    delay = np.arange(slots)[None, :] - np.arange(ROWS)[:, None]
-    filt = 0.0
-    for tap in range(ntaps):
-        here = jnp.asarray((delay == tap).astype(np.float32))
-        filt = filt + here[:, :, None] * taps[tap][None, None, :]
-    bank = jnp.asarray(waves)[:, :, None, None, :] * filt[None, None]
-    bank = bank.reshape(2, hop, window)
-    top = bank.astype(jnp.bfloat16)
-    rest = (bank - top.astype(jnp.float32)).astype(jnp.bfloat16)
-    bank = jnp.stack([top, rest], axis=1).reshape(4, hop, window)
+    waves = np.stack([np.cos(angle), np.sin(angle)]).swapaxes(1, 2) / math.sqrt(chans)
+    waves = np.tile(waves.astype(np.float32), (1, 1, window // chans))
+    tiled = jnp.tile(taps, (1, window // chans))
 
     spread = jnp.broadcast_to(positions.reshape(2, wide, 1, count), (2, wide, 2, count))
     quarter = np.zeros((1, wide, 2, count), np.float32)
@@ -456,9 +461,10 @@
             kernel, wide=wide, total=total, chans=chans, window=window, parts=parts
         ),
         out_shape=jax.ShapeDtypeStruct((share, chans, total // 4), jnp.float32),
-        in_specs=[vmem] * 5,
+        in_specs=[vmem] * 6,
         out_specs=vmem,
         scratch_shapes=[
+            pltpu.VMEM((4, hop, window), jnp.bfloat16),
             pltpu.VMEM((2 * LANES, padded), jnp.bfloat16),
             pltpu.VMEM((chans, total, LANES), jnp.bfloat16),
             pltpu.VMEM((total, width), jnp.bfloat16),
@@ -466,18 +472,24 @@
             pltpu.VMEM((beams, width), jnp.float32),
             pltpu.VMEM((2 * beams, width), jnp.bfloat16),
             pltpu.VMEM((2 * beams, total), jnp.bfloat16),
+            pltpu.VMEM((beams, width), jnp.float32),
+            pltpu.VMEM((8, width), jnp.float32),
+            pltpu.VMEM((chans, 8, LANES), jnp.float32),
+            pltpu.VMEM((wide, 8, LANES), jnp.float32),
             pltpu.VMEM((wide, share, total // 4), jnp.bfloat16),
             pltpu.VMEM((chans, share, total // 4), jnp.bfloat16),
             pltpu.SemaphoreType.DMA((parts, wide)),
             pltpu.SemaphoreType.DMA((parts, wide)),
-            pltpu.SemaphoreType.DMA((parts + 1,)),
+            pltpu.SemaphoreType.DMA((parts + 2,)),
+            pltpu.SemaphoreType.DMA((wide,)),
+            pltpu.SemaphoreType.DMA((wide,)),
             pltpu.SemaphoreType.DMA((wide,)),
             pltpu.SemaphoreType.DMA((wide,)),
         ],
         compiler_params=pltpu.CompilerParams(
             collective_id=0, has_side_effects=True, vmem_limit_bytes=48 * 2**20
         ),
-    )(volt, order, bank, place, cell)
+    )(voltages, order, jnp.asarray(waves), tiled, place, cell)
 
 
 def fits(voltages, taps, beam_index, wide):

time: 88.5 us -> 81.5 us (0.921)
  local copies, waits for them, and re-layouts: 19.9 us -> 5.08 us
  Pallas kernels: 66.9 us -> 73 us
  other arithmetic: 1.29 us -> 3.03 us
    mul x5 -> x0, local copies, waits for them, and re-layouts: 12.7 us -> none  [the longest x4 11.9 us: fused(): bank = jnp.asarray(waves)[:, :, None, None, :] * filt[None, None]]
    pallas_call x1, Pallas kernels: 66.9 us -> 73 us  [fused(): pl.pallas_call(functools.partial(kernel, wide=wide, total=total, chans=ch...]
    reshape x1 -> x0, local copies, waits for them, and re-layouts: 2.81 us -> none  [fused(): voltages.reshape(2 * count, length)]
    pad x1 -> x0, local copies, waits for them, and re-layouts: 1.8 us -> none  [fused(): jnp.pad(voltages.reshape(2 * count, length), ((0, 0), (0, padded - length)))]
    unnamed x15 -> x5, local copies, waits for them, and re-layouts: 1.92 us -> 3.05 us
    add x1 -> x0, other arithmetic: 1.01 us -> none  [fused(): filt = filt + here[:, :, None] * taps[tap][None, None, :]]
    convert_element_type x1, other arithmetic: 0.01 us -> 0.92 us  [fused(): order = (jnp.asarray(base) * keep[None, :]).astype(jnp.bfloat16)]
where the time goes in v1:
time: 81.5 us; the launch traced here: 81.2 us
  Pallas kernels  73 us (90%)
  local copies, waits for them, and re-layouts  5.08 us (6%)
  other arithmetic  3.03 us (4%)
    pallas_call x1, Pallas kernels, fused(): pl.pallas_call(functools.partial(kernel, wide=wide, total=total, chans=ch...  73 us
    unnamed x5, local copies, waits for them, and re-layouts  3.05 us

profile of v1, /device:TPU:0, one launch (start us, length us, event | category | flops | bytes accessed | tf_op | source)
XLA Modules:
  0.0 81.2 jit_solution(13517374383125313748)
XLA Ops:
  0.0 0.7 convert_element_type.12
  0.7 0.7 multiply_add_fusion.1
  1.4 0.8 broadcast_in_dim.11
  2.2 0.7 pad_maximum_fusion
  2.9 0.1 reshape.10.place_ref
  3.0 0.1 broadcast_in_dim.10
  3.1 0.1 mul.10
  3.2 0.7 tile.4
  3.9 0.1 tile.10.taps_ref
  4.0 0.9 %multiply_convert_fusion.order_ref = bf16[256,128]{1,0:T(8,128)(2,1)S(1)} fusion(f32[256,128]{1,0:T(8,128)} %constant.43.clone, f32[128]{0:T(128)S(1)} %mul.10), kind=kLoop, calls=%fused_computation | loop fusion | flops 65536 | bytes 197120 | tf_op jit(solution)/shard_map/convert_element_type | solution.py:438
  4.9 0.1 copy.11.cell_ref
  5.1 0.0 copy-start
  5.1 1.6 %copy-done = bf16[64,2,8240]{2,1,0:T(2,128)(2,1)S(1)} copy-done((bf16[64,2,8240]{2,1,0:T(2,128)(2,1)S(1)}, bf16[64,2,8240]{2,1,0:T(2,128)(2,1)}, u32[]{:S(2)}) %copy-start) | copy-done | bytes 2109464
  6.7 0.0 copy-start.1
  6.7 0.8 copy-done.1
  7.5 73.0 %shard_map.82 = f32[16,16,128]{2,1,0:T(8,128)S(1)} custom-call(bf16[64,2,8240]{2,1,0:T(2,128)(2,1)S(1)} %copy-done, bf16[256,128]{1,0:T(8,128)(2,1)S(1)} %multiply_convert_fusion.order_ref, f32[2,16,384]{2,1,0:T(8,128)S(1)} %copy-done.1, f32[4,384]{1,0:T(4,128)S(1)} %tile.10.taps_ref, f32[3,2048]{1,0:T(4,128)S(1)} %reshape.10.place_ref, ...), custom_call_target="tpu_custom_call" | custom-call | tf_op jit(solution)/shard_map/pallas_call | solution.py:459
  80.5 0.7 copy.13
  (2 shorter events, 0.0 us)
Async XLA Ops:
  5.1 1.6 %copy-start = (bf16[64,2,8240]{2,1,0:T(2,128)(2,1)S(1)}, bf16[64,2,8240]{2,1,0:T(2,128)(2,1)}, u32[]{:S(2)}) copy-start(bf16[64,2,8240]{2,1,0:T(2,128)(2,1)} %volt_ref.1) | copy-start | bytes 6328324
  6.7 0.8 copy-start.1

commit v2 on v1

--- a/solution.py
+++ b/solution.py
@@ -167,94 +167,125 @@
 
 
 def kernel(
-    volt_ref, order_ref, wave_ref, taps_ref, place_ref, cell_ref, out_ref,
-    bank, mixed, sent, spec, steer, weight, low, image, applied, scale,
+    volt_hbm, taps_ref, flags_ref, place_ref, index_ref, out_ref,
+    volt, bank, mixed, sent, spec, steer, weight, low, image, applied, scale,
     tell, told, give, got,
-    send_sem, recv_sem, own_sem, tell_sem, told_sem, give_sem, got_sem,
-    *, wide, total, chans, window, parts,
+    volt_sem, send_sem, recv_sem, tell_sem, told_sem, give_sem, got_sem,
+    *, wide, total, chans, window, bounds, early,
 ):
     me = lax.axis_index("wide")
-    peers = wide - 1
-    step = total // parts
-    beams = cell_ref.shape[0]
+    parts = len(bounds) - 1
+    beams = index_ref.shape[1]
     width = wide * LANES
     hop = ROWS * chans
-    length = volt_ref.shape[2]
+    length = volt_hbm.shape[2]
     ntaps = taps_ref.shape[0]
+    half_lanes = LANES // 2
 
     barrier = pltpu.get_barrier_semaphore()
+    fetch = pltpu.make_async_copy(volt_hbm, volt, volt_sem.at[0])
+    fetch.start()
+
+    def greet(off, carry):
+        pl.semaphore_signal(
+            barrier, inc=1, device_id={"wide": lax.rem(me + off, wide)}, device_id_type=MESH
+        )
+        return carry
+
+    lax.fori_loop(1, wide, greet, 0)
+
+    ranked = sorted(range(1, wide), key=lambda off: (abs(off - wide // 2), off))
+    cut = (len(ranked) + 1) // 2
+    mixed_order = [
+        entry for duo in zip(ranked[:cut], ranked[cut:] + [None]) for entry in duo
+    ]
+    mixed_order = [entry for entry in mixed_order if entry is not None]
+    turned_order = list(mixed_order)
+    for at in range(0, len(turned_order) - 1, 2):
+        turned_order[at], turned_order[at + 1] = turned_order[at + 1], turned_order[at]
 
     def everyone(act):
-        def body(off, carry):
-            act(lax.rem(me + off, wide))
-            return carry
-
-        lax.fori_loop(1, wide, body, 0)
-
-    everyone(
-        lambda other: pl.semaphore_signal(
-            barrier, inc=1, device_id={"wide": other}, device_id_type=MESH
-        )
-    )
-
-    slot = lax.broadcasted_iota(jnp.int32, (ROWS, window), 1) // chans
-    delay = slot - lax.broadcasted_iota(jnp.int32, (ROWS, window), 0)
+        core = lax.rem(me, 2)
+        for one, two in zip(mixed_order, turned_order):
+            act(lax.rem(me + (one + core * (two - one)), wide))
+
+    def iota(shape, axis):
+        return lax.broadcasted_iota(jnp.int32, shape, axis)
+
+    slot = iota((ROWS, window), 1) // chans
+    delay = slot - iota((ROWS, window), 0)
+    spread = jnp.where(iota((chans, window), 1) % chans == iota((chans, window), 0), 1.0, 0.0)
+    tiled = jnp.dot(
+        taps_ref[...], spread, precision=lax.Precision.HIGHEST, preferred_element_type=jnp.float32
+    )
     filt = jnp.zeros((ROWS, window), jnp.float32)
     for tap in range(ntaps):
-        filt = filt + jnp.where(delay == tap, taps_ref[tap : tap + 1, :], 0.0)
+        filt = filt + jnp.where(delay == tap, tiled[tap : tap + 1, :], 0.0)
+    spin = (iota((chans, window), 0) * (iota((chans, window), 1) % chans)) % chans
+    spin = spin.astype(jnp.float32) / chans
     for half in range(2):
+        wave = cosine_turns(spin - 0.25 * half) / math.sqrt(chans)
         for channel in range(chans):
-            rows = slice(channel * ROWS, (channel + 1) * ROWS)
-            entry = wave_ref[half, channel : channel + 1, :] * filt
+            entry = wave[channel : channel + 1, :] * filt
             top = entry.astype(jnp.bfloat16)
-            bank[2 * half, rows, :] = top
-            bank[2 * half + 1, rows, :] = (entry - top.astype(jnp.float32)).astype(jnp.bfloat16)
+            rest = (entry - top.astype(jnp.float32)).astype(jnp.bfloat16)
+            bank[half, channel * ROWS : (channel + 1) * ROWS, :] = top
+            bank[half, hop + channel * ROWS : hop + (channel + 1) * ROWS, :] = rest
+
+    doubled = jnp.where(iota((half_lanes, LANES), 1) // 2 == iota((half_lanes, LANES), 0), 1.0, 0.0)
+    keep = jnp.broadcast_to(flags_ref[...].astype(jnp.float32), (8, half_lanes))
+    keep = jnp.dot(
+        keep.astype(jnp.bfloat16), doubled.astype(jnp.bfloat16), preferred_element_type=jnp.float32
+    )[0:1]
+    row = iota((2 * LANES, LANES), 0)
+    antenna = row % half_lanes
+    quarter = row // half_lanes
+    from_part = jnp.where((quarter == 1) | (quarter == 2), 1, 0)
+    chosen = iota((2 * LANES, LANES), 1) == 2 * antenna + from_part
+    order = jnp.where(chosen, jnp.where(quarter == 3, -keep, keep), 0.0).astype(jnp.bfloat16)
 
     def mix(start, size):
-        volt = volt_ref[:, :, start : start + size].reshape(LANES, size)
+        block = volt[:, :, start : start + size].reshape(LANES, size)
         mixed[:, start : start + size] = jnp.dot(
-            order_ref[...], volt, preferred_element_type=jnp.float32
+            order, block, preferred_element_type=jnp.float32
         ).astype(jnp.bfloat16)
 
     def rows_of(part):
-        return pl.ds(pl.multiple_of(part * step, step), step)
+        return slice(bounds[part], bounds[part + 1])
 
     def lanes_of(block):
         return pl.ds(pl.multiple_of(block * LANES, LANES), LANES)
 
-    def spectra_copy(part, other, owner):
+    def remote(source, target, out_sem, in_sem, other):
         return pltpu.make_async_remote_copy(
-            src_ref=sent.at[other, rows_of(part), :],
-            dst_ref=spec.at[rows_of(part), lanes_of(owner)],
-            send_sem=send_sem.at[part, other],
-            recv_sem=recv_sem.at[part, owner],
+            src_ref=source,
+            dst_ref=target,
+            send_sem=out_sem,
+            recv_sem=in_sem,
             device_id={"wide": other},
             device_id_type=MESH,
         )
 
-    def own_copy(part):
-        return pltpu.make_async_copy(
-            sent.at[me, rows_of(part), :],
-            spec.at[rows_of(part), lanes_of(me)],
-            own_sem.at[part],
-        )
-
-    def tell_copy(other, owner):
-        return pltpu.make_async_remote_copy(
-            src_ref=tell.at[other],
-            dst_ref=told.at[owner],
-            send_sem=tell_sem.at[other],
-            recv_sem=told_sem.at[owner],
-            device_id={"wide": other},
-            device_id_type=MESH,
-        )
-
-    pairs = step // (2 * ROWS)
+    def await_bytes(ref, sem):
+        pltpu.make_async_copy(ref, ref, sem).wait()
+
+    def ship(part):
+        rows = rows_of(part)
+        everyone(
+            lambda other: remote(
+                sent.at[other, rows, :], spec.at[me, rows, :],
+                send_sem.at[part], recv_sem.at[part], other,
+            ).start()
+        )
+        pltpu.make_async_copy(
+            sent.at[me, rows, :], spec.at[me, rows, :], recv_sem.at[part]
+        ).start()
+
     tell[...] = jnp.zeros_like(tell)
 
     def channelize_pair(pair, carry):
         start = pl.multiple_of(pair * (2 * hop), LANES)
-        acc = jnp.zeros((hop, 2 * LANES), jnp.float32)
+        acc = jnp.zeros((2 * hop, 2 * LANES), jnp.float32)
         for half in range(2):
             rows = slice(half * LANES, (half + 1) * LANES)
             both = jnp.concatenate(
@@ -264,56 +295,72 @@
                 ],
                 axis=0,
             )
-            for piece in range(2):
-                acc = acc + lax.dot_general(
-                    bank[2 * half + piece], both, NT, preferred_element_type=jnp.float32
-                )
-        rounded = acc.astype(jnp.bfloat16)
+            acc = acc + lax.dot_general(
+                bank[half], both, NT, preferred_element_type=jnp.float32
+            )
+        rounded = (acc[:hop] + acc[hop:]).astype(jnp.bfloat16)
         for side in range(2):
-            row = pl.multiple_of(pair * (2 * ROWS) + side * ROWS, ROWS)
+            at = pl.multiple_of(pair * (2 * ROWS) + side * ROWS, ROWS)
             block = rounded[:, side * LANES : (side + 1) * LANES].reshape(chans, ROWS, LANES)
-            sent[:, pl.ds(row, ROWS), :] = block
+            sent[:, pl.ds(at, ROWS), :] = block
             block = block.astype(jnp.float32)
             block = block * block
             tell[...] += block[:, :8] + block[:, 8:]
         return carry
 
+    fetch.wait()
     tail = length // LANES * LANES
     mixed[:, tail:] = jnp.zeros((2 * LANES, mixed.shape[1] - tail), jnp.bfloat16)
     over = window - hop
     reach = 0
     for part in range(parts):
-        upto = min((part + 1) * step * chans + over, length)
+        upto = min(bounds[part + 1] * chans + over, length)
         mix(reach, upto - reach)
         reach = upto
-        lax.fori_loop(part * pairs, (part + 1) * pairs, channelize_pair, 0)
+        span = 2 * ROWS
+        lax.fori_loop(bounds[part] // span, bounds[part + 1] // span, channelize_pair, 0)
         if part == 0:
-            pl.semaphore_wait(barrier, peers)
-            everyone(lambda other: spectra_copy(0, other, me).start())
-            own_copy(0).start()
-    everyone(lambda other: tell_copy(other, me).start())
-    own_tell = pltpu.make_async_copy(tell.at[me], told.at[me], own_sem.at[parts])
-    own_tell.start()
-    for part in range(1, parts):
-        everyone(lambda other, part=part: spectra_copy(part, other, me).start())
-        own_copy(part).start()
-
+            pl.semaphore_wait(barrier, wide - 1)
+        if part < early:
+            ship(part)
+    everyone(
+        lambda other: remote(
+            tell.at[other], told.at[me], tell_sem.at[0], told_sem.at[0], other
+        ).start()
+    )
+    pltpu.make_async_copy(tell.at[me], told.at[me], told_sem.at[0]).start()
+    for part in range(early, parts):
+        ship(part)
+
+    index = index_ref[...]
     ratio = 1.0 + 0.5 * me.astype(jnp.float32) / chans
-    east = cell_ref[:, 0:1] * ratio
-    north = cell_ref[:, 1:2] * ratio
-
-    def steer_block(block, carry):
-        lanes = lanes_of(block)
-        turns = east * place_ref[0:1, lanes] + north * place_ref[1:2, lanes]
-        steer[:, lanes] = cosine_turns(turns + place_ref[2:3, lanes])
+    cells = [
+        ((index % grid_side).astype(jnp.float32) + 0.5) / grid_side - 0.5,
+        ((index // grid_side).astype(jnp.float32) + 0.5) / grid_side - 0.5,
+    ]
+    same = iota((beams, beams), 0) == iota((beams, beams), 1)
+    east, north = [
+        jnp.sum(jnp.where(same, cell, 0.0), axis=1, keepdims=True) * ratio for cell in cells
+    ]
+    first_half = iota((1, LANES), 1) < half_lanes
+    turn = jnp.where(first_half, 0.0, 0.25)
+
+    def steer_duo(duo, carry):
+        here = place_ref[:, lanes_of(duo)]
+        here = jnp.concatenate([here, jnp.zeros((6, LANES), jnp.float32)], axis=0)
+        there = swap_halves(here)
+        for side in range(2):
+            both = jnp.where(first_half, here, there) if side == 0 else jnp.where(
+                first_half, there, here
+            )
+            turns = east * both[0:1] + north * both[1:2] + turn
+            steer[:, lanes_of(2 * duo + side)] = cosine_turns(turns)
         return carry
 
-    lax.fori_loop(0, wide, steer_block, 0)
-
-    everyone(lambda other: tell_copy(other, other).wait_recv())
-    own_tell.wait()
-    lane = lax.broadcasted_iota(jnp.int32, (1, LANES), 1)
-    sign = jnp.where(lane < LANES // 2, 1.0, -1.0)
+    lax.fori_loop(0, wide // 2, steer_duo, 0)
+
+    await_bytes(told, told_sem.at[0])
+    sign = jnp.where(first_half, 1.0, -1.0)
     power = jnp.sum(told[...], axis=1, keepdims=True) * (1.0 / total)
     loading = jnp.sum(power) / (width // 2) + 1e-05
     for block in range(wide):
@@ -335,12 +382,13 @@
     lax.fori_loop(0, wide, first_block, 0)
 
     def project(rows):
-        return lax.dot_general(low[...], spec[rows, :], NT, preferred_element_type=jnp.float32)
+        strip = jnp.concatenate([spec[block, rows, :] for block in range(wide)], axis=1)
+        return lax.dot_general(low[...], strip, NT, preferred_element_type=jnp.float32)
 
     def back_project(rows, last, sweep, first):
         def duo_block(duo, carry):
-            span = pl.ds(pl.multiple_of(duo * (2 * LANES), 2 * LANES), 2 * LANES)
-            back = jnp.dot(image[:, rows], spec[rows, span], preferred_element_type=jnp.float32)
+            strip = jnp.concatenate([spec[2 * duo, rows, :], spec[2 * duo + 1, rows, :]], axis=1)
+            back = jnp.dot(image[:, rows], strip, preferred_element_type=jnp.float32)
             for side in range(2):
                 lanes = lanes_of(2 * duo + side)
                 cols = slice(side * LANES, (side + 1) * LANES)
@@ -361,17 +409,17 @@
 
         lax.fori_loop(0, wide // 2, duo_block, 0)
 
-    groups = [(0, 2), (2, 3), (3, 4)]
-    for begin, end in groups:
-        for part in range(begin, end):
-            everyone(lambda other, part=part: spectra_copy(part, other, other).wait_recv())
-            own_copy(part).wait()
-        rows = slice(begin * step, end * step)
+    for part in range(parts):
+        rows = rows_of(part)
+        await_bytes(spec.at[:, rows, :], recv_sem.at[part])
+        if bounds[part + 1] % LANES and part + 1 < parts:
+            continue
+        rows = slice(bounds[part] // LANES * LANES, bounds[part + 1])
         image[:, rows] = project(rows).astype(jnp.bfloat16)
-        back_project(rows, end == parts, 0, begin == 0)
+        back_project(rows, part + 1 == parts, 0, rows.start == 0)
 
     half_rows = total // 2
-    halves = [slice(cut * half_rows, (cut + 1) * half_rows) for cut in range(2)]
+    halves = [slice(half * half_rows, (half + 1) * half_rows) for half in range(2)]
     for sweep in range(1, ITERS):
         for rows in halves:
             image[:, rows] = project(rows).astype(jnp.bfloat16)
@@ -380,41 +428,32 @@
     group = total // 4
     share = give.shape[1]
     sums = jnp.zeros((beams, group), jnp.float32)
-    for cut, rows in enumerate(halves):
+    for half, rows in enumerate(halves):
         value = project(rows)
         energy = value[:beams] * value[:beams] + value[beams:] * value[beams:]
         energy = energy * (2.0 / width)
         top = energy.astype(jnp.bfloat16)
         rest = (energy - top.astype(jnp.float32)).astype(jnp.bfloat16)
-        source = lax.broadcasted_iota(jnp.int32, (half_rows, group), 0) + cut * half_rows
-        target = lax.broadcasted_iota(jnp.int32, (half_rows, group), 1) * 4
+        source = iota((half_rows, group), 0) + half * half_rows
+        target = iota((half_rows, group), 1) * 4
         pick = jnp.where((source >= target) & (source < target + 4), 1.0, 0.0)
         pick = pick.astype(jnp.bfloat16)
         sums = sums + jnp.dot(top, pick, preferred_element_type=jnp.float32)
         sums = sums + jnp.dot(rest, pick, preferred_element_type=jnp.float32)
     give[...] = sums.astype(jnp.bfloat16).reshape(wide, share, group)
-
-    def power_copy(other, owner):
-        return pltpu.make_async_remote_copy(
-            src_ref=give.at[other],
-            dst_ref=got.at[owner],
-            send_sem=give_sem.at[other],
-            recv_sem=got_sem.at[owner],
-            device_id={"wide": other},
-            device_id_type=MESH,
-        )
-
-    everyone(lambda other: power_copy(other, me).start())
-    mine = pltpu.make_async_copy(give.at[me], got.at[me], own_sem.at[parts + 1])
-    mine.start()
+    everyone(
+        lambda other: remote(
+            give.at[other], got.at[me], give_sem.at[0], got_sem.at[0], other
+        ).start()
+    )
+    pltpu.make_async_copy(give.at[me], got.at[me], got_sem.at[0]).start()
     for part in range(parts):
-        everyone(lambda other, part=part: spectra_copy(part, other, me).wait_send())
-    everyone(lambda other: tell_copy(other, me).wait_send())
-    everyone(lambda other: power_copy(other, other).wait_recv())
-    mine.wait()
+        await_bytes(sent.at[: wide - 1, rows_of(part), :], send_sem.at[part])
+    await_bytes(tell.at[: wide - 1], tell_sem.at[0])
+    await_bytes(got, got_sem.at[0])
     for channel in range(chans):
         out_ref[:, channel, :] = got[channel].astype(jnp.float32)
-    everyone(lambda other: power_copy(other, me).wait_send())
+    await_bytes(give.at[: wide - 1], give_sem.at[0])
 
 
 def fused(voltages, taps, flags, positions, beam_index):
@@ -426,48 +465,25 @@
     hop = ROWS * chans
     window = -(-(ROWS + ntaps - 1) * chans // LANES) * LANES
     padded = (total // ROWS - 1) * hop + window
-    parts = 4
-
-    antenna = np.arange(count)
-    base = np.zeros((4 * count, 2 * count), np.float32)
-    base[antenna, 2 * antenna] = 1.0
-    base[count + antenna, 2 * antenna + 1] = 1.0
-    base[2 * count + antenna, 2 * antenna + 1] = 1.0
-    base[3 * count + antenna, 2 * antenna] = -1.0
-    keep = jnp.repeat(flags.astype(jnp.float32), 2)
-    order = (jnp.asarray(base) * keep[None, :]).astype(jnp.bfloat16)
-
-    branch = np.arange(chans)
-    angle = 2.0 * math.pi / chans * (branch[:, None] * branch[None, :] % chans)
-    waves = np.stack([np.cos(angle), np.sin(angle)]).swapaxes(1, 2) / math.sqrt(chans)
-    waves = np.tile(waves.astype(np.float32), (1, 1, window // chans))
-    tiled = jnp.tile(taps, (1, window // chans))
-
-    spread = jnp.broadcast_to(positions.reshape(2, wide, 1, count), (2, wide, 2, count))
-    quarter = np.zeros((1, wide, 2, count), np.float32)
-    quarter[:, :, 1] = 0.25
-    place = jnp.concatenate([spread, jnp.asarray(quarter)]).reshape(3, wide * 2 * count)
-    column = (beam_index % grid_side).astype(jnp.float32)
-    row_cell = (beam_index // grid_side).astype(jnp.float32)
-    cell = jnp.stack(
-        [(column + 0.5) / grid_side - 0.5, (row_cell + 0.5) / grid_side - 0.5], axis=1
-    )
-
+    bounds = [0, LANES // 2] + list(range(LANES, total + 1, LANES))
+    parts = len(bounds) - 1
     share = beams // wide
     width = wide * LANES
     vmem = pl.BlockSpec(memory_space=pltpu.VMEM)
     return pl.pallas_call(
         functools.partial(
-            kernel, wide=wide, total=total, chans=chans, window=window, parts=parts
+            kernel, wide=wide, total=total, chans=chans, window=window, bounds=bounds,
+            early=min(3, parts),
         ),
         out_shape=jax.ShapeDtypeStruct((share, chans, total // 4), jnp.float32),
-        in_specs=[vmem] * 6,
+        in_specs=[pl.BlockSpec(memory_space=pl.ANY)] + [vmem] * 4,
         out_specs=vmem,
         scratch_shapes=[
-            pltpu.VMEM((4, hop, window), jnp.bfloat16),
+            pltpu.VMEM(voltages.shape, jnp.bfloat16),
+            pltpu.VMEM((2, 2 * hop, window), jnp.bfloat16),
             pltpu.VMEM((2 * LANES, padded), jnp.bfloat16),
             pltpu.VMEM((chans, total, LANES), jnp.bfloat16),
-            pltpu.VMEM((total, width), jnp.bfloat16),
+            pltpu.VMEM((wide, total, LANES), jnp.bfloat16),
             pltpu.VMEM((beams, width), jnp.float32),
             pltpu.VMEM((beams, width), jnp.float32),
             pltpu.VMEM((2 * beams, width), jnp.bfloat16),
@@ -478,18 +494,18 @@
             pltpu.VMEM((wide, 8, LANES), jnp.float32),
             pltpu.VMEM((wide, share, total // 4), jnp.bfloat16),
             pltpu.VMEM((chans, share, total // 4), jnp.bfloat16),
-            pltpu.SemaphoreType.DMA((parts, wide)),
-            pltpu.SemaphoreType.DMA((parts, wide)),
-            pltpu.SemaphoreType.DMA((parts + 2,)),
-            pltpu.SemaphoreType.DMA((wide,)),
-            pltpu.SemaphoreType.DMA((wide,)),
-            pltpu.SemaphoreType.DMA((wide,)),
-            pltpu.SemaphoreType.DMA((wide,)),
+            pltpu.SemaphoreType.DMA((1,)),
+            pltpu.SemaphoreType.DMA((parts,)),
+            pltpu.SemaphoreType.DMA((parts,)),
+            pltpu.SemaphoreType.DMA((1,)),
+            pltpu.SemaphoreType.DMA((1,)),
+            pltpu.SemaphoreType.DMA((1,)),
+            pltpu.SemaphoreType.DMA((1,)),
         ],
         compiler_params=pltpu.CompilerParams(
-            collective_id=0, has_side_effects=True, vmem_limit_bytes=48 * 2**20
+            collective_id=0, has_side_effects=True, vmem_limit_bytes=52 * 2**20
         ),
-    )(voltages, order, jnp.asarray(waves), tiled, place, cell)
+    )(voltages, taps, flags.reshape(1, -1), positions, beam_index.reshape(1, -1))
 
 
 def fits(voltages, taps, beam_index, wide):

time: 81.5 us -> 75.7 us (0.929)
  other arithmetic: 3.03 us -> 0 us
  local copies, waits for them, and re-layouts: 5.08 us -> 3.37 us
  Pallas kernels: 73 us -> 72.1 us
    convert_element_type x2 -> x0, other arithmetic: 1.57 us -> none  [the longest x1 0.92 us: fused(): order = (jnp.asarray(base) * keep[None, :]).astype(jnp.bfloat16)]
    pallas_call x1, Pallas kernels: 73 us -> 72.1 us  [fused(): pl.pallas_call(functools.partial(kernel, wide=wide, total=total, chans=ch...]
    another operation x3 -> x0, local copies, waits for them, and re-layouts: 0.91 us -> none  [the longest x2 0.78 us: fused(): tiled = jnp.tile(taps, (1, window // chans))]
    broadcast_in_dim x3 -> x0, local copies, waits for them, and re-layouts: 0.87 us -> none  [the longest x2 0.79 us: fused(): jnp.broadcast_to(positions.reshape(2, wide, 1, count), (2, wide, 2, count))]
    unnamed x5 -> x9, local copies, waits for them, and re-layouts: 3.05 us -> 3.37 us
where the time goes in v2:
time: 75.7 us; the launch traced here: 75.5 us
  Pallas kernels  72.1 us (95%)
  local copies, waits for them, and re-layouts  3.37 us (4%)
    pallas_call x1, Pallas kernels, fused(): pl.pallas_call(functools.partial(kernel, wide=wide, total=total, chans=ch...  72.1 us
    unnamed x9, local copies, waits for them, and re-layouts  3.37 us

profile of v2, /device:TPU:0, one launch (start us, length us, event | category | flops | bytes accessed | tf_op | source)
XLA Modules:
  0.0 75.5 jit_solution(6940922106553224092)
XLA Ops:
  0.0 0.0 copy-start
  0.0 0.7 copy-done
  0.7 0.0 copy-start.1
  0.7 0.7 copy-done.1
  1.4 0.0 copy-start.2
  1.4 0.7 copy-done.2
  2.1 0.0 copy-start.3
  2.1 0.7 copy-done.3
  2.7 72.1 %shard_map.55 = f32[16,16,128]{2,1,0:T(8,128)S(1)} custom-call(bf16[64,2,8240]{2,1,0:T(2,128)(2,1)} %volt_hbm.1, f32[4,16]{1,0:T(4,128)S(1)} %copy-done.1, s32[1,64]{1,0:T(1,128)S(1)} %bitcast.3, f32[2,1024]{1,0:T(2,128)S(1)} %copy-done, s32[1,256]{1,0:T(1,128)S(1)} %bitcast.2), custom_call_target="tpu_custom_call" | custom-call | tf_op jit(solution)/shard_map/pallas_call | solution.py:473
  74.8 0.7 copy.7
Async XLA Ops:
  0.0 0.7 copy-start
  0.7 0.7 copy-start.1
  1.4 0.7 copy-start.2
  2.1 0.7 copy-start.3

commit v3 on v2

--- a/solution.py
+++ b/solution.py
@@ -167,24 +167,38 @@
 
 
 def kernel(
-    volt_hbm, taps_ref, flags_ref, place_ref, index_ref, out_ref,
-    volt, bank, mixed, sent, spec, steer, weight, low, image, applied, scale,
+    volt_hbm, taps_hbm, flags_hbm, place_hbm, index_hbm, out_ref,
+    volt, taps_ref, flags_ref, place_ref, index_ref, bank, mixed, sent, spec, steer, weight, low, image, applied, scale,
     tell, told, give, got,
     volt_sem, send_sem, recv_sem, tell_sem, told_sem, give_sem, got_sem,
     *, wide, total, chans, window, bounds, early,
 ):
     me = lax.axis_index("wide")
     parts = len(bounds) - 1
-    beams = index_ref.shape[1]
+    beams = index_hbm.shape[1]
     width = wide * LANES
     hop = ROWS * chans
     length = volt_hbm.shape[2]
-    ntaps = taps_ref.shape[0]
+    ntaps = taps_hbm.shape[0]
     half_lanes = LANES // 2
 
     barrier = pltpu.get_barrier_semaphore()
-    fetch = pltpu.make_async_copy(volt_hbm, volt, volt_sem.at[0])
-    fetch.start()
+    first_reach = bounds[1] * chans + window - hop
+    loads = [
+        pltpu.make_async_copy(source, target, volt_sem.at[at])
+        for at, (source, target) in enumerate(
+            [
+                (taps_hbm, taps_ref),
+                (flags_hbm, flags_ref),
+                (place_hbm, place_ref),
+                (index_hbm, index_ref),
+                (volt_hbm.at[:, :, :first_reach], volt.at[:, :, :first_reach]),
+                (volt_hbm.at[:, :, first_reach:], volt.at[:, :, first_reach:]),
+            ]
+        )
+    ]
+    for load in loads:
+        load.start()
 
     def greet(off, carry):
         pl.semaphore_signal(
@@ -212,6 +226,8 @@
     def iota(shape, axis):
         return lax.broadcasted_iota(jnp.int32, shape, axis)
 
+    for load in loads[:4]:
+        load.wait()
     slot = iota((ROWS, window), 1) // chans
     delay = slot - iota((ROWS, window), 0)
     spread = jnp.where(iota((chans, window), 1) % chans == iota((chans, window), 0), 1.0, 0.0)
@@ -229,8 +245,9 @@
             entry = wave[channel : channel + 1, :] * filt
             top = entry.astype(jnp.bfloat16)
             rest = (entry - top.astype(jnp.float32)).astype(jnp.bfloat16)
-            bank[half, channel * ROWS : (channel + 1) * ROWS, :] = top
-            bank[half, hop + channel * ROWS : hop + (channel + 1) * ROWS, :] = rest
+            cols = slice(half * window, (half + 1) * window)
+            bank[channel * ROWS : (channel + 1) * ROWS, cols] = top
+            bank[hop + channel * ROWS : hop + (channel + 1) * ROWS, cols] = rest
 
     doubled = jnp.where(iota((half_lanes, LANES), 1) // 2 == iota((half_lanes, LANES), 0), 1.0, 0.0)
     keep = jnp.broadcast_to(flags_ref[...].astype(jnp.float32), (8, half_lanes))
@@ -285,19 +302,16 @@
 
     def channelize_pair(pair, carry):
         start = pl.multiple_of(pair * (2 * hop), LANES)
-        acc = jnp.zeros((2 * hop, 2 * LANES), jnp.float32)
-        for half in range(2):
-            rows = slice(half * LANES, (half + 1) * LANES)
-            both = jnp.concatenate(
-                [
-                    mixed[rows, pl.ds(start, window)],
-                    mixed[rows, pl.ds(pl.multiple_of(start + hop, LANES), window)],
-                ],
-                axis=0,
-            )
-            acc = acc + lax.dot_general(
-                bank[half], both, NT, preferred_element_type=jnp.float32
-            )
+        both = jnp.concatenate(
+            [
+                jnp.concatenate(
+                    [mixed[:LANES, pl.ds(at, window)], mixed[LANES:, pl.ds(at, window)]], axis=1
+                )
+                for at in (start, pl.multiple_of(start + hop, LANES))
+            ],
+            axis=0,
+        )
+        acc = lax.dot_general(bank[...], both, NT, preferred_element_type=jnp.float32)
         rounded = (acc[:hop] + acc[hop:]).astype(jnp.bfloat16)
         for side in range(2):
             at = pl.multiple_of(pair * (2 * ROWS) + side * ROWS, ROWS)
@@ -308,12 +322,14 @@
             tell[...] += block[:, :8] + block[:, 8:]
         return carry
 
-    fetch.wait()
+    loads[4].wait()
     tail = length // LANES * LANES
     mixed[:, tail:] = jnp.zeros((2 * LANES, mixed.shape[1] - tail), jnp.bfloat16)
     over = window - hop
     reach = 0
     for part in range(parts):
+        if part == 1:
+            loads[5].wait()
         upto = min(bounds[part + 1] * chans + over, length)
         mix(reach, upto - reach)
         reach = upto
@@ -412,9 +428,9 @@
     for part in range(parts):
         rows = rows_of(part)
         await_bytes(spec.at[:, rows, :], recv_sem.at[part])
-        if bounds[part + 1] % LANES and part + 1 < parts:
+        if bounds[part + 1] % (total // 2):
             continue
-        rows = slice(bounds[part] // LANES * LANES, bounds[part + 1])
+        rows = slice(bounds[part + 1] - total // 2, bounds[part + 1])
         image[:, rows] = project(rows).astype(jnp.bfloat16)
         back_project(rows, part + 1 == parts, 0, rows.start == 0)
 
@@ -476,11 +492,15 @@
             early=min(3, parts),
         ),
         out_shape=jax.ShapeDtypeStruct((share, chans, total // 4), jnp.float32),
-        in_specs=[pl.BlockSpec(memory_space=pl.ANY)] + [vmem] * 4,
+        in_specs=[pl.BlockSpec(memory_space=pl.ANY)] * 5,
         out_specs=vmem,
         scratch_shapes=[
             pltpu.VMEM(voltages.shape, jnp.bfloat16),
-            pltpu.VMEM((2, 2 * hop, window), jnp.bfloat16),
+            pltpu.VMEM(taps.shape, jnp.float32),
+            pltpu.VMEM((1, count), jnp.int32),
+            pltpu.VMEM(positions.shape, jnp.float32),
+            pltpu.VMEM((1, beams), jnp.int32),
+            pltpu.VMEM((2 * hop, 2 * window), jnp.bfloat16),
             pltpu.VMEM((2 * LANES, padded), jnp.bfloat16),
             pltpu.VMEM((chans, total, LANES), jnp.bfloat16),
             pltpu.VMEM((wide, total, LANES), jnp.bfloat16),
@@ -494,7 +514,7 @@
             pltpu.VMEM((wide, 8, LANES), jnp.float32),
             pltpu.VMEM((wide, share, total // 4), jnp.bfloat16),
             pltpu.VMEM((chans, share, total // 4), jnp.bfloat16),
-            pltpu.SemaphoreType.DMA((1,)),
+            pltpu.SemaphoreType.DMA((6,)),
             pltpu.SemaphoreType.DMA((parts,)),
             pltpu.SemaphoreType.DMA((parts,)),
             pltpu.SemaphoreType.DMA((1,)),
@@ -503,7 +523,7 @@
             pltpu.SemaphoreType.DMA((1,)),
         ],
         compiler_params=pltpu.CompilerParams(
-            collective_id=0, has_side_effects=True, vmem_limit_bytes=52 * 2**20
+            collective_id=0, has_side_effects=True, vmem_limit_bytes=64 * 2**20 - 2**16
         ),
     )(voltages, taps, flags.reshape(1, -1), positions, beam_index.reshape(1, -1))
 

time: 75.7 us -> 73.2 us (0.967)
  local copies, waits for them, and re-layouts: 3.37 us -> 1.57 us
    unnamed x9 -> x1, local copies, waits for them, and re-layouts: 3.37 us -> 1.57 us
where the time goes in v3:
time: 73.2 us; the launch traced here: 73.1 us
  Pallas kernels  71.5 us (98%)
  local copies, waits for them, and re-layouts  1.57 us (2%)
    pallas_call x1, Pallas kernels, fused(): pl.pallas_call(functools.partial(kernel, wide=wide, total=total, chans=ch...  71.5 us
    unnamed x1, local copies, waits for them, and re-layouts  1.57 us

profile of v3, /device:TPU:0, one launch (start us, length us, event | category | flops | bytes accessed | tf_op | source)
XLA Modules:
  0.0 73.1 jit_solution(191282417704786698)
XLA Ops:
  0.0 71.5 %shard_map.55 = f32[16,16,128]{2,1,0:T(8,128)} custom-call(bf16[64,2,8240]{2,1,0:T(2,128)(2,1)} %volt_hbm.1, f32[4,16]{1,0:T(4,128)} %taps_hbm.1, s32[1,64]{1,0:T(1,128)} %bitcast.3, f32[2,1024]{1,0:T(2,128)} %place_hbm.1, s32[1,256]{1,0:T(1,128)} %bitcast.2), custom_call_target="tpu_custom_call" | custom-call | tf_op jit(solution)/shard_map/pallas_call | solution.py:489
  71.5 1.6 %copy.7 = f32[16,16,128]{2,1,0:T(8,128)} copy(f32[16,16,128]{2,1,0:T(8,128)} %shard_map.55) | data formatting | bytes 262144

commit v4 on v3

--- a/solution.py
+++ b/solution.py
@@ -149,6 +149,7 @@
 MESH = pl.DeviceIdType.MESH
 LANES = 128
 ROWS = 16
+CHUNK = 256
 NT = (((1,), (1,)), ((), ()))
 
 
@@ -168,13 +169,13 @@
 
 def kernel(
     volt_hbm, taps_hbm, flags_hbm, place_hbm, index_hbm, out_ref,
-    volt, taps_ref, flags_ref, place_ref, index_ref, bank, mixed, sent, spec, steer, weight, low, image, applied, scale,
+    volt, taps_ref, flags_ref, place_ref, index_ref, bank, order, mixed, sent, spec, steer, weight, low, whole, image, applied, scale, sums,
     tell, told, give, got,
     volt_sem, send_sem, recv_sem, tell_sem, told_sem, give_sem, got_sem,
-    *, wide, total, chans, window, bounds, early,
+    *, wide, total, chans, window, parts, early,
 ):
     me = lax.axis_index("wide")
-    parts = len(bounds) - 1
+    step = total // parts
     beams = index_hbm.shape[1]
     width = wide * LANES
     hop = ROWS * chans
@@ -183,7 +184,7 @@
     half_lanes = LANES // 2
 
     barrier = pltpu.get_barrier_semaphore()
-    first_reach = bounds[1] * chans + window - hop
+    first_reach = min(step * chans + CHUNK, length // CHUNK * CHUNK)
     loads = [
         pltpu.make_async_copy(source, target, volt_sem.at[at])
         for at, (source, target) in enumerate(
@@ -208,20 +209,13 @@
 
     lax.fori_loop(1, wide, greet, 0)
 
-    ranked = sorted(range(1, wide), key=lambda off: (abs(off - wide // 2), off))
-    cut = (len(ranked) + 1) // 2
-    mixed_order = [
-        entry for duo in zip(ranked[:cut], ranked[cut:] + [None]) for entry in duo
-    ]
-    mixed_order = [entry for entry in mixed_order if entry is not None]
-    turned_order = list(mixed_order)
-    for at in range(0, len(turned_order) - 1, 2):
-        turned_order[at], turned_order[at + 1] = turned_order[at + 1], turned_order[at]
-
     def everyone(act):
-        core = lax.rem(me, 2)
-        for one, two in zip(mixed_order, turned_order):
-            act(lax.rem(me + (one + core * (two - one)), wide))
+        def body(turn, carry):
+            off = 1 + lax.rem((turn + lax.rem(me, 2)) * (wide // 2 - 1), wide - 1)
+            act(lax.rem(me + off, wide))
+            return carry
+
+        lax.fori_loop(0, wide - 1, body, 0)
 
     def iota(shape, axis):
         return lax.broadcasted_iota(jnp.int32, shape, axis)
@@ -259,16 +253,21 @@
     quarter = row // half_lanes
     from_part = jnp.where((quarter == 1) | (quarter == 2), 1, 0)
     chosen = iota((2 * LANES, LANES), 1) == 2 * antenna + from_part
-    order = jnp.where(chosen, jnp.where(quarter == 3, -keep, keep), 0.0).astype(jnp.bfloat16)
+    order[...] = jnp.where(chosen, jnp.where(quarter == 3, -keep, keep), 0.0).astype(jnp.bfloat16)
 
     def mix(start, size):
-        block = volt[:, :, start : start + size].reshape(LANES, size)
-        mixed[:, start : start + size] = jnp.dot(
-            order, block, preferred_element_type=jnp.float32
+        lanes = pl.ds(start, size)
+        block = volt[:, :, lanes].reshape(LANES, size)
+        mixed[:, lanes] = jnp.dot(
+            order[...], block, preferred_element_type=jnp.float32
         ).astype(jnp.bfloat16)
 
+    def mix_chunk(chunk, carry):
+        mix(pl.multiple_of(chunk * CHUNK, CHUNK), CHUNK)
+        return carry
+
     def rows_of(part):
-        return slice(bounds[part], bounds[part + 1])
+        return pl.ds(pl.multiple_of(part * step, step), step)
 
     def lanes_of(block):
         return pl.ds(pl.multiple_of(block * LANES, LANES), LANES)
@@ -322,31 +321,48 @@
             tell[...] += block[:, :8] + block[:, 8:]
         return carry
 
+    chunks = length // CHUNK
+    tail = chunks * CHUNK
     loads[4].wait()
-    tail = length // LANES * LANES
     mixed[:, tail:] = jnp.zeros((2 * LANES, mixed.shape[1] - tail), jnp.bfloat16)
-    over = window - hop
-    reach = 0
-    for part in range(parts):
-        if part == 1:
+    lead = first_reach // CHUNK
+    ahead = step * chans // CHUNK
+    lax.fori_loop(0, lead - ahead, mix_chunk, 0)
+
+    def produce(part, carry):
+        @pl.when(part == 1)
+        def _():
             loads[5].wait()
-        upto = min(bounds[part + 1] * chans + over, length)
-        mix(reach, upto - reach)
-        reach = upto
-        span = 2 * ROWS
-        lax.fori_loop(bounds[part] // span, bounds[part + 1] // span, channelize_pair, 0)
-        if part == 0:
+            mix(tail, length - tail)
+
+        begin = jnp.minimum(lead - ahead + part * ahead, chunks)
+        lax.fori_loop(begin, jnp.minimum(begin + ahead, chunks), mix_chunk, 0)
+        pairs = step // (2 * ROWS)
+        lax.fori_loop(part * pairs, (part + 1) * pairs, channelize_pair, 0)
+
+        @pl.when(part == 0)
+        def _():
             pl.semaphore_wait(barrier, wide - 1)
-        if part < early:
+
+        @pl.when(part < early)
+        def _():
             ship(part)
+
+        return carry
+
+    lax.fori_loop(0, parts, produce, 0)
     everyone(
         lambda other: remote(
             tell.at[other], told.at[me], tell_sem.at[0], told_sem.at[0], other
         ).start()
     )
     pltpu.make_async_copy(tell.at[me], told.at[me], told_sem.at[0]).start()
-    for part in range(early, parts):
+
+    def ship_late(part, carry):
         ship(part)
+        return carry
+
+    lax.fori_loop(early, parts, ship_late, 0)
 
     index = index_ref[...]
     ratio = 1.0 + 0.5 * me.astype(jnp.float32) / chans
@@ -397,74 +413,90 @@
 
     lax.fori_loop(0, wide, first_block, 0)
 
-    def project(rows):
-        strip = jnp.concatenate([spec[block, rows, :] for block in range(wide)], axis=1)
-        return lax.dot_general(low[...], strip, NT, preferred_element_type=jnp.float32)
-
-    def back_project(rows, last, sweep, first):
-        def duo_block(duo, carry):
-            strip = jnp.concatenate([spec[2 * duo, rows, :], spec[2 * duo + 1, rows, :]], axis=1)
-            back = jnp.dot(image[:, rows], strip, preferred_element_type=jnp.float32)
-            for side in range(2):
-                lanes = lanes_of(2 * duo + side)
-                cols = slice(side * LANES, (side + 1) * LANES)
-                fresh = back[:beams, cols] - sign * swap_halves(back[beams:, cols])
-                if not first:
-                    fresh = applied[:, lanes] + fresh
-                if not last:
-                    applied[:, lanes] = fresh
-                    continue
-                value = weight[:, lanes]
-                value = value + scale[0:1, lanes] * (
-                    steer[:, lanes] - (fresh * (1.0 / total) + loading * value)
-                )
-                if sweep < ITERS - 1:
-                    weight[:, lanes] = value
-                keep_low(lanes, value)
-            return carry
-
-        lax.fori_loop(0, wide // 2, duo_block, 0)
-
-    for part in range(parts):
-        rows = rows_of(part)
-        await_bytes(spec.at[:, rows, :], recv_sem.at[part])
-        if bounds[part + 1] % (total // 2):
-            continue
-        rows = slice(bounds[part + 1] - total // 2, bounds[part + 1])
-        image[:, rows] = project(rows).astype(jnp.bfloat16)
-        back_project(rows, part + 1 == parts, 0, rows.start == 0)
-
     half_rows = total // 2
-    halves = [slice(half * half_rows, (half + 1) * half_rows) for half in range(2)]
-    for sweep in range(1, ITERS):
-        for rows in halves:
-            image[:, rows] = project(rows).astype(jnp.bfloat16)
-        back_project(slice(0, total), True, sweep, True)
-
     group = total // 4
     share = give.shape[1]
-    sums = jnp.zeros((beams, group), jnp.float32)
-    for half, rows in enumerate(halves):
-        value = project(rows)
-        energy = value[:beams] * value[:beams] + value[beams:] * value[beams:]
-        energy = energy * (2.0 / width)
-        top = energy.astype(jnp.bfloat16)
-        rest = (energy - top.astype(jnp.float32)).astype(jnp.bfloat16)
-        source = iota((half_rows, group), 0) + half * half_rows
-        target = iota((half_rows, group), 1) * 4
-        pick = jnp.where((source >= target) & (source < target + 4), 1.0, 0.0)
-        pick = pick.astype(jnp.bfloat16)
-        sums = sums + jnp.dot(top, pick, preferred_element_type=jnp.float32)
-        sums = sums + jnp.dot(rest, pick, preferred_element_type=jnp.float32)
-    give[...] = sums.astype(jnp.bfloat16).reshape(wide, share, group)
+
+    def stage_half(turn, carry):
+        stage = turn // 2
+        half = turn % 2
+        rows = pl.ds(pl.multiple_of(half * half_rows, half_rows), half_rows)
+
+        @pl.when(stage == 0)
+        def _():
+            def land(part, carry):
+                await_bytes(spec.at[:, rows_of(part), :], recv_sem.at[part])
+                return carry
+
+            lax.fori_loop(half * (parts // 2), (half + 1) * (parts // 2), land, 0)
+
+        strip = jnp.concatenate([spec[block, rows, :] for block in range(wide)], axis=1)
+        whole[...] = lax.dot_general(low[...], strip, NT, preferred_element_type=jnp.float32)
+
+        @pl.when(stage < ITERS)
+        def _():
+            image[...] = whole[...].astype(jnp.bfloat16)
+
+            def duo_block(duo, carry):
+                strip = jnp.concatenate(
+                    [spec[2 * duo, rows, :], spec[2 * duo + 1, rows, :]], axis=1
+                )
+                back = jnp.dot(image[...], strip, preferred_element_type=jnp.float32)
+                for side in range(2):
+                    lanes = lanes_of(2 * duo + side)
+                    cols = slice(side * LANES, (side + 1) * LANES)
+                    fresh = back[:beams, cols] - sign * swap_halves(back[beams:, cols])
+
+                    @pl.when(half == 0)
+                    def _():
+                        applied[:, lanes] = fresh
+
+                    @pl.when(half == 1)
+                    def _():
+                        value = weight[:, lanes]
+                        value = value + scale[0:1, lanes] * (
+                            steer[:, lanes]
+                            - ((applied[:, lanes] + fresh) * (1.0 / total) + loading * value)
+                        )
+                        weight[:, lanes] = value
+                        keep_low(lanes, value)
+
+                return carry
+
+            lax.fori_loop(0, wide // 2, duo_block, 0)
+
+        @pl.when(stage == ITERS)
+        def _():
+            value = whole[...]
+            energy = value[:beams] * value[:beams] + value[beams:] * value[beams:]
+            energy = energy * (2.0 / width)
+            top = energy.astype(jnp.bfloat16)
+            rest = (energy - top.astype(jnp.float32)).astype(jnp.bfloat16)
+            source = iota((half_rows, group), 0) + half * half_rows
+            target = iota((half_rows, group), 1) * 4
+            pick = jnp.where((source >= target) & (source < target + 4), 1.0, 0.0)
+            pick = pick.astype(jnp.bfloat16)
+            sums[...] += jnp.dot(top, pick, preferred_element_type=jnp.float32) + jnp.dot(
+                rest, pick, preferred_element_type=jnp.float32
+            )
+
+        return carry
+
+    sums[...] = jnp.zeros_like(sums)
+    lax.fori_loop(0, 2 * (ITERS + 1), stage_half, 0)
+    give[...] = sums[...].astype(jnp.bfloat16).reshape(wide, share, group)
     everyone(
         lambda other: remote(
             give.at[other], got.at[me], give_sem.at[0], got_sem.at[0], other
         ).start()
     )
     pltpu.make_async_copy(give.at[me], got.at[me], got_sem.at[0]).start()
-    for part in range(parts):
+
+    def settle(part, carry):
         await_bytes(sent.at[: wide - 1, rows_of(part), :], send_sem.at[part])
+        return carry
+
+    lax.fori_loop(0, parts, settle, 0)
     await_bytes(tell.at[: wide - 1], tell_sem.at[0])
     await_bytes(got, got_sem.at[0])
     for channel in range(chans):
@@ -481,15 +513,14 @@
     hop = ROWS * chans
     window = -(-(ROWS + ntaps - 1) * chans // LANES) * LANES
     padded = (total // ROWS - 1) * hop + window
-    bounds = [0, LANES // 2] + list(range(LANES, total + 1, LANES))
-    parts = len(bounds) - 1
+    parts = 8
     share = beams // wide
     width = wide * LANES
     vmem = pl.BlockSpec(memory_space=pltpu.VMEM)
     return pl.pallas_call(
         functools.partial(
-            kernel, wide=wide, total=total, chans=chans, window=window, bounds=bounds,
-            early=min(3, parts),
+            kernel, wide=wide, total=total, chans=chans, window=window, parts=parts,
+            early=parts // 2,
         ),
         out_shape=jax.ShapeDtypeStruct((share, chans, total // 4), jnp.float32),
         in_specs=[pl.BlockSpec(memory_space=pl.ANY)] * 5,
@@ -501,15 +532,18 @@
             pltpu.VMEM(positions.shape, jnp.float32),
             pltpu.VMEM((1, beams), jnp.int32),
             pltpu.VMEM((2 * hop, 2 * window), jnp.bfloat16),
+            pltpu.VMEM((2 * LANES, LANES), jnp.bfloat16),
             pltpu.VMEM((2 * LANES, padded), jnp.bfloat16),
             pltpu.VMEM((chans, total, LANES), jnp.bfloat16),
             pltpu.VMEM((wide, total, LANES), jnp.bfloat16),
             pltpu.VMEM((beams, width), jnp.float32),
             pltpu.VMEM((beams, width), jnp.float32),
             pltpu.VMEM((2 * beams, width), jnp.bfloat16),
-            pltpu.VMEM((2 * beams, total), jnp.bfloat16),
+            pltpu.VMEM((2 * beams, total // 2), jnp.float32),
+            pltpu.VMEM((2 * beams, total // 2), jnp.bfloat16),
             pltpu.VMEM((beams, width), jnp.float32),
             pltpu.VMEM((8, width), jnp.float32),
+            pltpu.VMEM((beams, total // 4), jnp.float32),
             pltpu.VMEM((chans, 8, LANES), jnp.float32),
             pltpu.VMEM((wide, 8, LANES), jnp.float32),
             pltpu.VMEM((wide, share, total // 4), jnp.bfloat16),
@@ -535,9 +569,11 @@
     return (
         2 * count == LANES
         and chans == wide
-        and (ROWS * chans) % LANES == 0
+        and ROWS * chans == CHUNK
+        and length % CHUNK < LANES
+        and (ntaps - 1) * chans <= CHUNK
         and wide % 2 == 0
-        and total % 256 == 0
+        and total % (16 * ROWS) == 0
         and beam_index.shape[0] % (ROWS * wide) == 0
         and (total // 4) % LANES == 0
     )

time: 73.2 us -> 80.3 us (1.097)
  Pallas kernels: 71.5 us -> 78.6 us
    pallas_call x1, Pallas kernels: 71.5 us -> 78.6 us  [fused(): pl.pallas_call(functools.partial(kernel, wide=wide, total=total, chans=ch...]
where the time goes in v4:
time: 80.3 us; the launch traced here: 80.1 us
  Pallas kernels  78.6 us (98%)
  local copies, waits for them, and re-layouts  1.57 us (2%)
    pallas_call x1, Pallas kernels, fused(): pl.pallas_call(functools.partial(kernel, wide=wide, total=total, chans=ch...  78.6 us

profile of v4, /device:TPU:0, one launch (start us, length us, event | category | flops | bytes accessed | tf_op | source)
XLA Modules:
  0.0 80.1 jit_solution(16758811588034709150)
XLA Ops:
  0.0 78.6 %shard_map.55 = f32[16,16,128]{2,1,0:T(8,128)} custom-call(bf16[64,2,8240]{2,1,0:T(2,128)(2,1)} %volt_hbm.1, f32[4,16]{1,0:T(4,128)} %taps_hbm.1, s32[1,64]{1,0:T(1,128)} %bitcast.3, f32[2,1024]{1,0:T(2,128)} %place_hbm.1, s32[1,256]{1,0:T(1,128)} %bitcast.2), custom_call_target="tpu_custom_call" | custom-call | tf_op jit(solution)/shard_map/pallas_call | solution.py:520
  78.6 1.6 %copy.7 = f32[16,16,128]{2,1,0:T(8,128)} copy(f32[16,16,128]{2,1,0:T(8,128)} %shard_map.55) | data formatting | bytes 262144

commit v5 on v3

--- a/solution.py
+++ b/solution.py
@@ -178,7 +178,7 @@
     beams = index_hbm.shape[1]
     width = wide * LANES
     hop = ROWS * chans
-    length = volt_hbm.shape[2]
+    length = volt_hbm.shape[1]
     ntaps = taps_hbm.shape[0]
     half_lanes = LANES // 2
 
@@ -192,8 +192,8 @@
                 (flags_hbm, flags_ref),
                 (place_hbm, place_ref),
                 (index_hbm, index_ref),
-                (volt_hbm.at[:, :, :first_reach], volt.at[:, :, :first_reach]),
-                (volt_hbm.at[:, :, first_reach:], volt.at[:, :, first_reach:]),
+                (volt_hbm.at[:, :first_reach], volt.at[:, :first_reach]),
+                (volt_hbm.at[:, first_reach:], volt.at[:, first_reach:]),
             ]
         )
     ]
@@ -262,7 +262,7 @@
     order = jnp.where(chosen, jnp.where(quarter == 3, -keep, keep), 0.0).astype(jnp.bfloat16)
 
     def mix(start, size):
-        block = volt[:, :, start : start + size].reshape(LANES, size)
+        block = volt[:, start : start + size]
         mixed[:, start : start + size] = jnp.dot(
             order, block, preferred_element_type=jnp.float32
         ).astype(jnp.bfloat16)
@@ -495,7 +495,7 @@
         in_specs=[pl.BlockSpec(memory_space=pl.ANY)] * 5,
         out_specs=vmem,
         scratch_shapes=[
-            pltpu.VMEM(voltages.shape, jnp.bfloat16),
+            pltpu.VMEM((2 * count, length), jnp.bfloat16),
             pltpu.VMEM(taps.shape, jnp.float32),
             pltpu.VMEM((1, count), jnp.int32),
             pltpu.VMEM(positions.shape, jnp.float32),
@@ -525,7 +525,7 @@
         compiler_params=pltpu.CompilerParams(
             collective_id=0, has_side_effects=True, vmem_limit_bytes=64 * 2**20 - 2**16
         ),
-    )(voltages, taps, flags.reshape(1, -1), positions, beam_index.reshape(1, -1))
+    )(voltages.reshape(2 * count, length), taps, flags.reshape(1, -1), positions, beam_index.reshape(1, -1))
 
 
 def fits(voltages, taps, beam_index, wide):

time: 73.2 us -> 77.8 us (1.063)
  local copies, waits for them, and re-layouts: 1.57 us -> 6.09 us
    reshape x0 -> x1, local copies, waits for them, and re-layouts: none -> 4.52 us  [fused(): voltages.reshape(2 * count, length)]
where the time goes in v5:
time: 77.8 us; the launch traced here: 77.6 us
  Pallas kernels  71.5 us (92%)
  local copies, waits for them, and re-layouts  6.09 us (8%)
    pallas_call x1, Pallas kernels, fused(): pl.pallas_call(functools.partial(kernel, wide=wide, total=total, chans=ch...  71.5 us
    reshape x1, local copies, waits for them, and re-layouts, fused(): voltages.reshape(2 * count, length)  4.52 us
    unnamed x1, local copies, waits for them, and re-layouts  1.57 us

profile of v5, /device:TPU:0, one launch (start us, length us, event | category | flops | bytes accessed | tf_op | source)
XLA Modules:
  0.0 77.6 jit_solution(6123349021140000853)
XLA Ops:
  0.0 4.5 %reshape.9.volt_hbm = bf16[128,8240]{1,0:T(8,128)(2,1)} reshape(bf16[64,2,8240]{2,1,0:T(2,128)(2,1)} %param.5) | data formatting | bytes 4218880 | tf_op jit(solution)/shard_map/reshape | solution.py:528
  4.5 71.5 %shard_map.55 = f32[16,16,128]{2,1,0:T(8,128)} custom-call(bf16[128,8240]{1,0:T(8,128)(2,1)} %reshape.9.volt_hbm, f32[4,16]{1,0:T(4,128)} %taps_hbm.1, s32[1,64]{1,0:T(1,128)} %bitcast.3, f32[2,1024]{1,0:T(2,128)} %place_hbm.1, s32[1,256]{1,0:T(1,128)} %bitcast.2), custom_call_target="tpu_custom_call" | custom-call | tf_op jit(solution)/shard_map/pallas_call | solution.py:489
  76.0 1.6 %copy.7 = f32[16,16,128]{2,1,0:T(8,128)} copy(f32[16,16,128]{2,1,0:T(8,128)} %shard_map.55) | data formatting | bytes 262144

commit v6 on v3

--- a/solution.py
+++ b/solution.py
@@ -481,7 +481,7 @@
     hop = ROWS * chans
     window = -(-(ROWS + ntaps - 1) * chans // LANES) * LANES
     padded = (total // ROWS - 1) * hop + window
-    bounds = [0, LANES // 2] + list(range(LANES, total + 1, LANES))
+    bounds = [0, LANES // 2, total // 2, total]
     parts = len(bounds) - 1
     share = beams // wide
     width = wide * LANES
@@ -489,7 +489,7 @@
     return pl.pallas_call(
         functools.partial(
             kernel, wide=wide, total=total, chans=chans, window=window, bounds=bounds,
-            early=min(3, parts),
+            early=2,
         ),
         out_shape=jax.ShapeDtypeStruct((share, chans, total // 4), jnp.float32),
         in_specs=[pl.BlockSpec(memory_space=pl.ANY)] * 5,

time: 73.2 us -> 72.7 us (level)
  no operation moved by 1% of the time
where the time goes in v6:
time: 72.7 us; the launch traced here: 72.6 us
  Pallas kernels  71 us (98%)
  local copies, waits for them, and re-layouts  1.57 us (2%)
    pallas_call x1, Pallas kernels, fused(): pl.pallas_call(functools.partial(kernel, wide=wide, total=total, chans=ch...  71 us
    unnamed x1, local copies, waits for them, and re-layouts  1.57 us

profile of v6, /device:TPU:0, one launch (start us, length us, event | category | flops | bytes accessed | tf_op | source)
XLA Modules:
  0.0 72.6 jit_solution(3030180577597324812)
XLA Ops:
  0.0 71.0 %shard_map.55 = f32[16,16,128]{2,1,0:T(8,128)} custom-call(bf16[64,2,8240]{2,1,0:T(2,128)(2,1)} %volt_hbm.1, f32[4,16]{1,0:T(4,128)} %taps_hbm.1, s32[1,64]{1,0:T(1,128)} %bitcast.3, f32[2,1024]{1,0:T(2,128)} %place_hbm.1, s32[1,256]{1,0:T(1,128)} %bitcast.2), custom_call_target="tpu_custom_call" | custom-call | tf_op jit(solution)/shard_map/pallas_call | solution.py:489
  71.0 1.6 %copy.7 = f32[16,16,128]{2,1,0:T(8,128)} copy(f32[16,16,128]{2,1,0:T(8,128)} %shard_map.55) | data formatting | bytes 262144

commit v7 on v6

--- a/solution.py
+++ b/solution.py
@@ -302,17 +302,23 @@
 
     def channelize_pair(pair, carry):
         start = pl.multiple_of(pair * (2 * hop), LANES)
-        both = jnp.concatenate(
-            [
-                jnp.concatenate(
-                    [mixed[:LANES, pl.ds(at, window)], mixed[LANES:, pl.ds(at, window)]], axis=1
+        acc = jnp.zeros((hop, 2 * LANES), jnp.float32)
+        for half in range(2):
+            rows = slice(half * LANES, (half + 1) * LANES)
+            cols = slice(half * window, (half + 1) * window)
+            both = jnp.concatenate(
+                [
+                    mixed[rows, pl.ds(start, window)],
+                    mixed[rows, pl.ds(pl.multiple_of(start + hop, LANES), window)],
+                ],
+                axis=0,
+            )
+            for piece in range(2):
+                acc = acc + lax.dot_general(
+                    bank[piece * hop : (piece + 1) * hop, cols], both, NT,
+                    preferred_element_type=jnp.float32,
                 )
-                for at in (start, pl.multiple_of(start + hop, LANES))
-            ],
-            axis=0,
-        )
-        acc = lax.dot_general(bank[...], both, NT, preferred_element_type=jnp.float32)
-        rounded = (acc[:hop] + acc[hop:]).astype(jnp.bfloat16)
+        rounded = acc.astype(jnp.bfloat16)
         for side in range(2):
             at = pl.multiple_of(pair * (2 * ROWS) + side * ROWS, ROWS)
             block = rounded[:, side * LANES : (side + 1) * LANES].reshape(chans, ROWS, LANES)
@@ -481,7 +487,7 @@
     hop = ROWS * chans
     window = -(-(ROWS + ntaps - 1) * chans // LANES) * LANES
     padded = (total // ROWS - 1) * hop + window
-    bounds = [0, LANES // 2, total // 2, total]
+    bounds = [0, total // 8, total // 4, total // 2, 3 * total // 4, 7 * total // 8, total]
     parts = len(bounds) - 1
     share = beams // wide
     width = wide * LANES
@@ -489,7 +495,7 @@
     return pl.pallas_call(
         functools.partial(
             kernel, wide=wide, total=total, chans=chans, window=window, bounds=bounds,
-            early=2,
+            early=parts - 1,
         ),
         out_shape=jax.ShapeDtypeStruct((share, chans, total // 4), jnp.float32),
         in_specs=[pl.BlockSpec(memory_space=pl.ANY)] * 5,

time: 72.7 us -> 77 us (1.059)
  Pallas kernels: 71 us -> 75.3 us
    pallas_call x1, Pallas kernels: 71 us -> 75.3 us  [fused(): pl.pallas_call(functools.partial(kernel, wide=wide, total=total, chans=ch...]
where the time goes in v7:
time: 77 us; the launch traced here: 76.9 us
  Pallas kernels  75.3 us (98%)
  local copies, waits for them, and re-layouts  1.57 us (2%)
    pallas_call x1, Pallas kernels, fused(): pl.pallas_call(functools.partial(kernel, wide=wide, total=total, chans=ch...  75.3 us
    unnamed x1, local copies, waits for them, and re-layouts  1.57 us

profile of v7, /device:TPU:0, one launch (start us, length us, event | category | flops | bytes accessed | tf_op | source)
XLA Modules:
  0.0 76.9 jit_solution(4044899443824160385)
XLA Ops:
  0.0 75.3 %shard_map.55 = f32[16,16,128]{2,1,0:T(8,128)} custom-call(bf16[64,2,8240]{2,1,0:T(2,128)(2,1)} %volt_hbm.1, f32[4,16]{1,0:T(4,128)} %taps_hbm.1, s32[1,64]{1,0:T(1,128)} %bitcast.3, f32[2,1024]{1,0:T(2,128)} %place_hbm.1, s32[1,256]{1,0:T(1,128)} %bitcast.2), custom_call_target="tpu_custom_call" | custom-call | tf_op jit(solution)/shard_map/pallas_call | solution.py:495
  75.3 1.6 %copy.7 = f32[16,16,128]{2,1,0:T(8,128)} copy(f32[16,16,128]{2,1,0:T(8,128)} %shard_map.55) | data formatting | bytes 262144
